TPU v7x, 256 devices: a whole 4x4x8 slice. The times are simulated.
256 devices in a mesh: row: 8 (over z_lo, core), col: 32 (over y, z_hi, x).
Axes of the slice: x: 4, y: 4, z: 8 (z_hi: 2, z_lo: 4; z = z_hi * 4 + z_lo), core: 2. Of those that a mesh axis runs over, the one named last changes fastest.
Arguments:
- activations: bfloat16 [1024, 8192], P(('row', 'col')), may hold values from -6 to 6
- cotangent: bfloat16 [1024, 8192], P(('row', 'col')), may hold values from -1.5 to 1.5
- up_panels: bfloat16 [16, 128, 128, 128], P('row', 'col'), may hold values from -0.125 to 0.125
- down_panels: bfloat16 [16, 128, 128, 128], P('row', 'col'), may hold values from -0.09375 to 0.09375
- block_index: int32 [128, 16], P('col'), may hold values from 0 to 63, as said below
- block_count: int32 [128], P('col'), may hold values from 5 to 16, as said below
Outputs:
- outputs: bfloat16 [1024, 8192], P(('row', 'col'))
- grad_inputs: bfloat16 [1024, 8192], P(('row', 'col'))
- grad_up: bfloat16 [16, 128, 128, 128], P('row', 'col')
- grad_down: bfloat16 [16, 128, 128, 128], P('row', 'col')
Inputs may be any that keep to these rules, and one draw needn't show every extreme that they name: `block_index`: the 16 block numbers of one panel are distinct. `block_count`: some panel has all 16 slots live.
All inputs are finite; a program needn't handle non-finite values.
Results may differ from a plain program's by a relative error of at most 0.024.
Values may be sent and summed in bfloat16 or wider, within the bound.
No kernel may reach another device: no remote copies, remote signals or barrier semaphores. Data moves between devices by JAX's collectives and lax.ppermute only.
A program may use at most 128 MiB of HBM per device.

v0:
```python
import functools

import jax
import jax.numpy as jnp
from jax import lax
from jax.experimental import pallas as pl
from jax.experimental.pallas import tpu as pltpu
from jax.sharding import PartitionSpec as P

BLK = 128
NX, NY, NH, NL, NC = 4, 4, 2, 4, 2
NZ = NH * NL
BF = jnp.bfloat16
F32 = jnp.float32
NT = (((1,), (1,)), ((), ()))
TN = (((0,), (0,)), ((), ()))
HOPS = (0, 1, 2, 3, -1, -2, -3, 4)


def device(z, core, y, x):
    z = z % NZ
    row = (z % NL) * NC + core % NC
    col = ((y % NY) * NH + z // NL) * NX + x % NX
    return row * NY * NH * NX + col


def send(value, dz=0, dc=0, dy=0, dx=0):
    pairs = [
        (device(z, c, y, x), device(z + dz, c + dc, y + dy, x + dx))
        for z in range(NZ)
        for c in range(NC)
        for y in range(NY)
        for x in range(NX)
    ]
    return lax.ppermute(value, ("row", "col"), pairs)


def swap_cores(value):
    return send(value, dc=1)


def after(values, *others):
    return lax.optimization_barrier((values, others))[0]


def total(terms):
    result = terms[0].astype(F32)
    for term in terms[1:]:
        result = result + term.astype(F32)
    return result


def products_kernel(slots, *refs):
    place, index, count = refs[:3]
    rows_in, weights_in = refs[3:5], refs[5:14]
    grads_out, sums_out = refs[14:23], refs[23:25]
    act, cot, weights, grads, out_sum, in_sum, sums, a_cat, c_cat, up_cat, down_cat = refs[25:36]
    row_sems, weight_sems, grad_sems, sum_sems = refs[36:]
    rows = act.shape[0]
    half = rows // 2
    z = place[0]
    own = z // NL
    hops = HOPS[:7] + (4, 4)
    arrivals = []
    for o in range(2):
        span = pl.ds(o * half, half)
        arrivals.append(pltpu.make_async_copy(rows_in[o].at[0], act.at[span], row_sems.at[o]))
        arrivals.append(pltpu.make_async_copy(rows_in[o].at[1], cot.at[span], row_sems.at[2 + o]))
    for copy in arrivals:
        copy.start()
    near, loads, stores = [], [], []
    for n, hop in enumerate(hops):
        there = (z + hop + NZ) % NZ
        spots = weights.at[there], grads.at[there]
        if hop == 4:
            spots = [spot.at[pl.ds(8 * (n - 7), 8)] for spot in spots]
        near.append(there // NL == own)
        loads.append(pltpu.make_async_copy(weights_in[n], spots[0], weight_sems.at[n]))
        stores.append(pltpu.make_async_copy(spots[1], grads_out[n], grad_sems.at[n]))
    for n in range(9):
        pl.when(near[n])(loads[n].start)
    for n in range(9):
        pl.when(jnp.logical_not(near[n]))(loads[n].start)
    out_sum[...] = jnp.zeros_like(out_sum)
    in_sum[...] = jnp.zeros_like(in_sum)
    for copy in arrivals:
        copy.wait()
    for n in range(9):
        pl.when(near[n])(loads[n].wait)
    leaving = []
    for n in range(4):
        far, p = n // 2, n % 2
        base = (1 - own if far else own) * NL
        live = count[n]
        if n == 2:
            for m in range(9):
                pl.when(jnp.logical_not(near[m]))(loads[m].wait)
                pl.when(near[m])(stores[m].start)
        for k in range(slots):
            lanes = pl.ds(pl.multiple_of(index[n, k] * BLK, BLK), BLK)
            here = slice(k * BLK, (k + 1) * BLK)
            a_cat[:, here] = act[:, lanes]
            c_cat[:, here] = cot[:, lanes]
            up = weights[base + k // 4, k % 4 * 4 + p * 2]
            down = weights[base + k // 4, k % 4 * 4 + p * 2 + 1]
            up_cat[here, :] = jnp.where(k < live, up, jnp.zeros_like(up))
            down_cat[:, here] = jnp.where(k < live, down, jnp.zeros_like(down))
        preact = jnp.dot(a_cat[...], up_cat[...], preferred_element_type=F32)
        grad_hidden = lax.dot_general(c_cat[...], down_cat[...], NT, preferred_element_type=F32)
        gate = jax.nn.sigmoid(preact)
        hidden = (preact * gate).astype(BF)
        derivative = gate * (1.0 + preact * (1.0 - gate))
        grad_pre = (grad_hidden * derivative).astype(BF)
        spread = jnp.dot(hidden, down_cat[...], preferred_element_type=F32)
        spread_in = lax.dot_general(grad_pre, up_cat[...], NT, preferred_element_type=F32)
        for k in range(slots):
            lanes = pl.ds(pl.multiple_of(index[n, k] * BLK, BLK), BLK)
            here = slice(k * BLK, (k + 1) * BLK)
            out_sum[:, lanes] += spread[:, here]
            in_sum[:, lanes] += spread_in[:, here]
        if n == 3:
            for o in (1, 0):
                for m, total_rows in enumerate((out_sum, in_sum)):
                    sums[o, m] = total_rows[o * half : (o + 1) * half, :].astype(BF)
                copy = pltpu.make_async_copy(sums.at[o], sums_out[o], sum_sems.at[o])
                copy.start()
                leaving.append(copy)
        up_grad = lax.dot_general(a_cat[...], grad_pre, TN, preferred_element_type=F32)
        down_grad = lax.dot_general(hidden, c_cat[...], TN, preferred_element_type=F32)
        for k in range(slots):
            here = slice(k * BLK, (k + 1) * BLK)
            spot = k % 4 * 4 + p * 2
            grads[base + k // 4, spot] = jnp.where(k < live, up_grad[here, :], 0.0).astype(BF)
            grads[base + k // 4, spot + 1] = jnp.where(k < live, down_grad[:, here], 0.0).astype(BF)
    for m in range(9):
        pl.when(jnp.logical_not(near[m]))(stores[m].start)
    for copy in leaving + stores:
        copy.wait()


def products(place, index, count, row_pair, weights):
    panels, slots = index.shape
    _, half, features = row_pair[0].shape
    shard = weights[0].shape
    rows, wide = 2 * half, slots * BLK
    any_space = pl.BlockSpec(memory_space=pl.ANY)
    smem = pl.BlockSpec(memory_space=pltpu.SMEM)
    shapes = [part.shape for part in weights] + [(2, half, features)] * 2
    results = pl.pallas_call(
        functools.partial(products_kernel, slots),
        out_shape=[jax.ShapeDtypeStruct(shape, BF) for shape in shapes],
        in_specs=[smem] * 3 + [any_space] * 11,
        out_specs=[any_space] * 11,
        scratch_shapes=[
            pltpu.VMEM((rows, features), BF),
            pltpu.VMEM((rows, features), BF),
            pltpu.VMEM((NZ,) + shard, BF),
            pltpu.VMEM((NZ,) + shard, BF),
            pltpu.VMEM((rows, features), F32),
            pltpu.VMEM((rows, features), F32),
            pltpu.VMEM((2, 2, half, features), BF),
            pltpu.VMEM((rows, wide), BF),
            pltpu.VMEM((rows, wide), BF),
            pltpu.VMEM((wide, BLK), BF),
            pltpu.VMEM((BLK, wide), BF),
            pltpu.SemaphoreType.DMA((4,)),
            pltpu.SemaphoreType.DMA((9,)),
            pltpu.SemaphoreType.DMA((9,)),
            pltpu.SemaphoreType.DMA((2,)),
        ],
        compiler_params=pltpu.CompilerParams(vmem_limit_bytes=60 * 2**20),
        cost_estimate=pl.CostEstimate(flops=1_700_000_000, bytes_accessed=16_000_000, transcendentals=65536),
    )(place, index, count, *row_pair, *weights)
    return results[:9], results[9:]


def ring_gather(shard):
    up, down = [shard], [shard]
    for _ in range(3):
        up.append(send(up[-1], dz=-1))
        down.append(send(down[-1], dz=1))
    half = shard.shape[0] // 2
    across = [send(up[-1][:half], dz=-1), send(down[-1][half:], dz=1)]
    return [shard] + up[1:] + down[1:] + across


def pair(up, down):
    return send(up, dz=1), send(down, dz=-1)


def cut(value, parts, axis=0):
    size = value.shape[axis] // parts
    return [lax.slice_in_dim(value, d * size, (d + 1) * size, axis=axis) for d in range(parts)]


def add_half(part, arrived, which):
    size = arrived.shape[0]
    room = [(which * size, (1 - which) * size)] + [(0, 0)] * (part.ndim - 1)
    return (part.astype(F32) + jnp.pad(arrived.astype(F32), room)).astype(BF)


def shards(activations, cotangent, up_panels, down_panels, block_index, block_count):
    row, col = lax.axis_index("row"), lax.axis_index("col")
    core, low, high = row % NC, row // NC, (col // NX) % NH
    own_first = core == 0

    lists = jnp.concatenate([block_index, block_count[:, None]], axis=1)
    far_lists = send(lists, dz=4)
    lists = lax.dynamic_slice_in_dim(jnp.stack([lists, far_lists]), 2 * core, 2, axis=1).reshape(4, -1)
    index, count = lists[:, :-1], lists[:, -1]
    place = (high * NL + low).astype(jnp.int32).reshape(1)

    both = jnp.stack([up_panels, down_panels], axis=2)
    keep = lax.dynamic_slice_in_dim(both, 2 * core, 2, axis=1)
    got = swap_cores(lax.dynamic_slice_in_dim(both, 2 - 2 * core, 2, axis=1))
    shard = jnp.where(own_first, jnp.stack([keep, got]), jnp.stack([got, keep]))
    weights = ring_gather(shard.reshape(-1, BLK, BLK))

    rows = jnp.stack([activations, cotangent])
    rows = [rows] + [send(rows, dx=-d) for d in (1, 2, 3)]
    rows = jnp.concatenate(after(rows, far_lists, weights[1], weights[4]), axis=1)
    rows = after([rows] + [send(rows, dy=-d) for d in (1, 2, 3)], weights[3], weights[6])
    rows = jnp.concatenate(rows, axis=1)
    row_pair = [rows, swap_cores(rows)]

    parts, (own, far) = products(place, index, count, row_pair, weights)
    step_1 = pair(parts[7], parts[8])
    up = add_half(parts[3], step_1[0], 0)
    down = add_half(parts[6], step_1[1], 1)
    step_2 = pair(up, down)

    far = swap_cores(far)
    sums = [total(both).astype(BF) for both in zip(cut(own, 4, 1), cut(far, 4, 1))]
    first = [send(sums[1], dy=1), send(sums[3], dy=3)]

    up = total([parts[2], step_2[0]]).astype(BF)
    down = total([parts[5], step_2[1]]).astype(BF)
    step_3 = pair(*after([up, down], *first))
    second = send(after(sums[2], *first), dy=2)

    up = total([parts[1], step_3[0]]).astype(BF)
    down = total([parts[4], step_3[1]]).astype(BF)
    step_4 = pair(*after([up, down], second))
    sums = after([sums[0], *first, second], *step_3)
    sums = cut(total(sums).astype(BF), 4, 1)
    sums = after([sums[0]] + [send(sums[d], dx=d) for d in (1, 2, 3)], *step_4)
    sums = total(sums).astype(BF)

    cores = total([parts[0], *step_4]).astype(BF).reshape(2, 2, 2, 2, BLK, BLK)
    mine = lax.dynamic_index_in_dim(cores, core, 0, keepdims=False)
    other = swap_cores(lax.dynamic_index_in_dim(cores, 1 - core, 0, keepdims=False))
    grads = jnp.where(
        own_first, jnp.concatenate([mine, other], axis=1), jnp.concatenate([other, mine], axis=1)
    )
    return sums[0], sums[1], grads[:, :, 0], grads[:, :, 1]


def solution(mesh):
    tokens = P(("row", "col"), None)
    blocks = P("row", "col", None, None)
    in_specs = (tokens, tokens, blocks, blocks, P("col", None), P("col"))
    out_specs = (tokens, tokens, blocks, blocks)
    return jax.shard_map(shards, mesh=mesh, in_specs=in_specs, out_specs=out_specs, check_vma=False)
```

profile of v0, /device:TPU:2, one launch (start us, length us, event | category | flops | bytes accessed | tf_op | source)
XLA Modules:
  0.0 143.6 jit_solution(16876604261024430481)
XLA Ops:
  3.5 7.2 %collective-permute-start = (s32[4,17]{1,0:T(4,128)S(1)}, s32[4,17]{1,0:T(4,128)S(1)}, u32[]{:S(2)}, u32[]{:S(2)}) collective-permute-start(s32[4,17]{1,0:T(4,128)S(1)} %pad_add_fusion), channel_id=1, source_target_pairs={{0,4},{1,5},{2,6},{3,7},{8,12},{9,13},{10,14},{11,15},{16,20},{17,... | collective-permute-start | bytes 824 | tf_op jit(solution)/shard_map/ppermute | solution.py:35
  11.0 1.9 %collective-permute-start.6 = (bf16[16,128,128]{2,1,0:T(8,128)(2,1)S(1)}, bf16[16,128,128]{2,1,0:T(8,128)(2,1)S(1)}, u32[]{:S(2)}, u32[]{:S(2)}) collective-permute-start(bf16[16,128,128]{2,1,0:T(8,128)(2,1)S(1)} %bitcast.31), channel_id=1, source_target_pairs={{0,64},{1,65},{2,66},{3,67},{8,72},{9,73},{10,74},{11,75},{16,80},... | collective-permute-start | bytes 1572872 | tf_op jit(solution)/shard_map/ppermute | solution.py:35
  13.6 2.4 %collective-permute-start.2 = (bf16[2,4,8192]{2,1,0:T(4,128)(2,1)S(1)}, bf16[2,4,8192]{2,1,0:T(4,128)(2,1)S(1)}, u32[]{:S(2)}, u32[]{:S(2)}) collective-permute-start(bf16[2,4,8192]{2,1,0:T(4,128)(2,1)S(1)} %pad_maximum_fusion.1), channel_id=1, source_target_pairs={{0,2},{1,3},{2,0},{3,1},{8,10},{9,11},{10,8},{11,9},{16,18},{17,19... | collective-permute-start | bytes 393224 | tf_op jit(solution)/shard_map/ppermute | solution.py:35
  16.0 1.8 %collective-permute-start.3 = (bf16[2,4,8192]{2,1,0:T(4,128)(2,1)S(1)}, bf16[2,4,8192]{2,1,0:T(4,128)(2,1)S(1)}, u32[]{:S(2)}, u32[]{:S(2)}) collective-permute-start(bf16[2,4,8192]{2,1,0:T(4,128)(2,1)S(1)} %pad_maximum_fusion.1), channel_id=1, source_target_pairs={{0,1},{1,2},{2,3},{3,0},{8,9},{9,10},{10,11},{11,8},{16,17},{17,18... | collective-permute-start | bytes 393224 | tf_op jit(solution)/shard_map/ppermute | solution.py:35
  18.6 3.3 %collective-permute-done.2 = bf16[2,4,8192]{2,1,0:T(4,128)(2,1)S(1)} collective-permute-done((bf16[2,4,8192]{2,1,0:T(4,128)(2,1)S(1)}, bf16[2,4,8192]{2,1,0:T(4,128)(2,1)S(1)}, u32[]{:S(2)}, u32[]{:S(2)}) %collective-permute-start.2) | collective-permute-done | bytes 131104 | tf_op jit(solution)/shard_map/ppermute | solution.py:35
  22.7 2.2 %collective-permute-done.5.refs_6_ = bf16[16,128,128]{2,1,0:T(8,128)(2,1)S(1)} collective-permute-done((bf16[16,128,128]{2,1,0:T(8,128)(2,1)S(1)}, bf16[16,128,128]{2,1,0:T(8,128)(2,1)S(1)}, u32[]{:S(2)}, u32[]{:S(2)}) %collective-permute-start.5) | collective-permute-done | bytes 524320 | tf_op jit(solution)/shard_map/ppermute | solution.py:35
  24.9 1.3 collective-permute-done.6.refs_9_
  26.6 1.7 %collective-permute-start.12 = (bf16[16,128,128]{2,1,0:T(8,128)(2,1)S(1)}, bf16[16,128,128]{2,1,0:T(8,128)(2,1)S(1)}, u32[]{:S(2)}, u32[]{:S(2)}) collective-permute-start(bf16[16,128,128]{2,1,0:T(8,128)(2,1)S(1)} %collective-permute-done.6.refs_9_), channel_id=1, source_target_pairs={{0,64},{1,65},{2,66},{3,67},{8,72},{9,73},{10,74},{11,75},{16,80},... | collective-permute-start | bytes 1572872 | tf_op jit(solution)/shard_map/ppermute | solution.py:35
  28.6 3.1 %collective-permute-start.7 = (bf16[2,16,8192]{2,1,0:T(8,128)(2,1)S(1)}, bf16[2,16,8192]{2,1,0:T(8,128)(2,1)S(1)}, u32[]{:S(2)}, u32[]{:S(2)}) collective-permute-start(bf16[2,16,8192]{2,1,0:T(8,128)(2,1)S(1)} %pad_maximum_fusion), channel_id=1, source_target_pairs={{0,24},{1,25},{2,26},{3,27},{8,0},{9,1},{10,2},{11,3},{16,8},{17,9... | collective-permute-start | bytes 1572872 | tf_op jit(solution)/shard_map/ppermute | solution.py:35
  33.2 6.2 %collective-permute-done.10.refs_7_ = bf16[16,128,128]{2,1,0:T(8,128)(2,1)S(1)} collective-permute-done((bf16[16,128,128]{2,1,0:T(8,128)(2,1)S(1)}, bf16[16,128,128]{2,1,0:T(8,128)(2,1)S(1)}, u32[]{:S(2)}, u32[]{:S(2)}) %collective-permute-start.10) | collective-permute-done | bytes 524320 | tf_op jit(solution)/shard_map/ppermute | solution.py:35
  39.4 1.8 %collective-permute-start.11 = (bf16[16,128,128]{2,1,0:T(8,128)(2,1)S(1)}, bf16[16,128,128]{2,1,0:T(8,128)(2,1)S(1)}, u32[]{:S(2)}, u32[]{:S(2)}) collective-permute-start(bf16[16,128,128]{2,1,0:T(8,128)(2,1)S(1)} %collective-permute-done.10.refs_7_), channel_id=1, source_target_pairs={{0,196},{1,197},{2,198},{3,199},{8,204},{9,205},{10,206},{11,207},... | collective-permute-start | bytes 1572872 | tf_op jit(solution)/shard_map/ppermute | solution.py:35
  41.5 11.5 %collective-permute-done.7 = bf16[2,16,8192]{2,1,0:T(8,128)(2,1)S(1)} collective-permute-done((bf16[2,16,8192]{2,1,0:T(8,128)(2,1)S(1)}, bf16[2,16,8192]{2,1,0:T(8,128)(2,1)S(1)}, u32[]{:S(2)}, u32[]{:S(2)}) %collective-permute-start.7) | collective-permute-done | bytes 524320 | tf_op jit(solution)/shard_map/ppermute | solution.py:35
  53.0 3.7 %collective-permute-done.9 = bf16[2,16,8192]{2,1,0:T(8,128)(2,1)S(1)} collective-permute-done((bf16[2,16,8192]{2,1,0:T(8,128)(2,1)S(1)}, bf16[2,16,8192]{2,1,0:T(8,128)(2,1)S(1)}, u32[]{:S(2)}, u32[]{:S(2)}) %collective-permute-start.9) | collective-permute-done | bytes 524320 | tf_op jit(solution)/shard_map/ppermute | solution.py:35
  57.6 1.9 %collective-permute-start.15 = (bf16[8,128,128]{2,1,0:T(8,128)(2,1)S(1)}, bf16[8,128,128]{2,1,0:T(8,128)(2,1)S(1)}, u32[]{:S(2)}, u32[]{:S(2)}) collective-permute-start(bf16[8,128,128]{2,1,0:T(8,128)(2,1)S(1)} %slice.80), channel_id=1, source_target_pairs={{0,196},{1,197},{2,198},{3,199},{8,204},{9,205},{10,206},{11,207},... | collective-permute-start | bytes 786440 | tf_op jit(solution)/shard_map/ppermute | solution.py:35
  60.8 5.1 %collective-permute-done.15.refs_12_ = bf16[8,128,128]{2,1,0:T(8,128)(2,1)S(1)} collective-permute-done((bf16[8,128,128]{2,1,0:T(8,128)(2,1)S(1)}, bf16[8,128,128]{2,1,0:T(8,128)(2,1)S(1)}, u32[]{:S(2)}, u32[]{:S(2)}) %collective-permute-start.15) | collective-permute-done | bytes 262176 | tf_op jit(solution)/shard_map/ppermute | solution.py:35
  65.9 3.0 %collective-permute-done.16.refs_13_ = bf16[8,128,128]{2,1,0:T(8,128)(2,1)S(1)} collective-permute-done((bf16[8,128,128]{2,1,0:T(8,128)(2,1)S(1)}, bf16[8,128,128]{2,1,0:T(8,128)(2,1)S(1)}, u32[]{:S(2)}, u32[]{:S(2)}) %collective-permute-start.16) | collective-permute-done | bytes 262176 | tf_op jit(solution)/shard_map/ppermute | solution.py:35
  69.7 13.1 %shard_map.93 = (bf16[16,128,128]{2,1,0:T(8,128)(2,1)}, bf16[16,128,128]{2,1,0:T(8,128)(2,1)}, bf16[16,128,128]{2,1,0:T(8,128)(2,1)}, bf16[16,128,128]{2,1,0:T(8...) custom-call(s32[1]{0:T(128)} %bitcast.refs_0_, ...), custom_call_target="tpu_custom_call" | custom-call | flops 1700000000 | bytes 16000000 | tf_op jit(solution)/shard_map/pallas_call | solution.py:149
  83.0 2.0 %collective-permute-start.21 = (bf16[8,128,128]{2,1,0:T(8,128)(2,1)}, bf16[8,128,128]{2,1,0:T(8,128)(2,1)S(1)}, u32[]{:S(2)}, u32[]{:S(2)}) collective-permute-start(bf16[8,128,128]{2,1,0:T(8,128)(2,1)} %get-tuple-element.49), channel_id=1, source_target_pairs={{0,64},{1,65},{2,66},{3,67},{8,72},{9,73},{10,74},{11,75},{16,80},... | collective-permute-start | bytes 786440 | tf_op jit(solution)/shard_map/ppermute | solution.py:35
  85.0 6.8 %collective-permute-done.23 = bf16[8,128,128]{2,1,0:T(8,128)(2,1)S(1)} collective-permute-done((bf16[8,128,128]{2,1,0:T(8,128)(2,1)}, bf16[8,128,128]{2,1,0:T(8,128)(2,1)S(1)}, u32[]{:S(2)}, u32[]{:S(2)}) %collective-permute-start.23) | collective-permute-done | bytes 262176 | tf_op jit(solution)/shard_map/ppermute | solution.py:35
  93.0 1.6 %collective-permute-start.24 = (bf16[16,128,128]{2,1,0:T(8,128)(2,1)S(1)}, bf16[16,128,128]{2,1,0:T(8,128)(2,1)S(1)}, u32[]{:S(2)}, u32[]{:S(2)}) collective-permute-start(bf16[16,128,128]{2,1,0:T(8,128)(2,1)S(1)} %add_convert_fusion.5), channel_id=1, source_target_pairs={{0,196},{1,197},{2,198},{3,199},{8,204},{9,205},{10,206},{11,207},... | collective-permute-start | bytes 1572872 | tf_op jit(solution)/shard_map/ppermute | solution.py:35
  96.9 3.2 %collective-permute-start.19 = (bf16[2,16,8192]{2,1,0:T(8,128)(2,1)S(1)}, bf16[2,16,8192]{2,1,0:T(8,128)(2,1)S(1)}, u32[]{:S(2)}, u32[]{:S(2)}) collective-permute-start(bf16[2,16,8192]{2,1,0:T(8,128)(2,1)S(1)} %get-tuple-element.69), channel_id=1, source_target_pairs={{0,24},{1,25},{2,26},{3,27},{8,0},{9,1},{10,2},{11,3},{16,8},{17,9... | collective-permute-start | bytes 1572872 | tf_op jit(solution)/shard_map/ppermute | solution.py:35
  100.1 6.4 %collective-permute-done.24 = bf16[16,128,128]{2,1,0:T(8,128)(2,1)S(1)} collective-permute-done((bf16[16,128,128]{2,1,0:T(8,128)(2,1)S(1)}, bf16[16,128,128]{2,1,0:T(8,128)(2,1)S(1)}, u32[]{:S(2)}, u32[]{:S(2)}) %collective-permute-start.24) | collective-permute-done | bytes 524320 | tf_op jit(solution)/shard_map/ppermute | solution.py:35
  107.5 2.9 %collective-permute-done.22 = bf16[16,128,128]{2,1,0:T(8,128)(2,1)S(1)} collective-permute-done((bf16[16,128,128]{2,1,0:T(8,128)(2,1)S(1)}, bf16[16,128,128]{2,1,0:T(8,128)(2,1)S(1)}, u32[]{:S(2)}, u32[]{:S(2)}) %collective-permute-start.22) | collective-permute-done | bytes 524320 | tf_op jit(solution)/shard_map/ppermute | solution.py:35
  111.3 2.6 %collective-permute-start.26 = (bf16[16,128,128]{2,1,0:T(8,128)(2,1)}, bf16[16,128,128]{2,1,0:T(8,128)(2,1)}, u32[]{:S(2)}, u32[]{:S(2)}) collective-permute-start(bf16[16,128,128]{2,1,0:T(8,128)(2,1)} %add_convert_fusion.4), channel_id=1, source_target_pairs={{0,196},{1,197},{2,198},{3,199},{8,204},{9,205},{10,206},{11,207},... | collective-permute-start | bytes 1572872 | tf_op jit(solution)/shard_map/ppermute | solution.py:35
  113.9 1.5 %collective-permute-start.20 = (bf16[2,16,8192]{2,1,0:T(8,128)(2,1)S(1)}, bf16[2,16,8192]{2,1,0:T(8,128)(2,1)S(1)}, u32[]{:S(2)}, u32[]{:S(2)}) collective-permute-start(bf16[2,16,8192]{2,1,0:T(8,128)(2,1)S(1)} %get-tuple-element.46), channel_id=1, source_target_pairs={{0,16},{1,17},{2,18},{3,19},{8,24},{9,25},{10,26},{11,27},{16,0},{... | collective-permute-start | bytes 1572872 | tf_op jit(solution)/shard_map/ppermute | solution.py:35
  115.3 8.7 %collective-permute-done.26 = bf16[16,128,128]{2,1,0:T(8,128)(2,1)} collective-permute-done((bf16[16,128,128]{2,1,0:T(8,128)(2,1)}, bf16[16,128,128]{2,1,0:T(8,128)(2,1)}, u32[]{:S(2)}, u32[]{:S(2)}) %collective-permute-start.26) | collective-permute-done | bytes 524320 | tf_op jit(solution)/shard_map/ppermute | solution.py:35
  125.2 2.0 %collective-permute-done.25 = bf16[16,128,128]{2,1,0:T(8,128)(2,1)} collective-permute-done((bf16[16,128,128]{2,1,0:T(8,128)(2,1)}, bf16[16,128,128]{2,1,0:T(8,128)(2,1)}, u32[]{:S(2)}, u32[]{:S(2)}) %collective-permute-start.25) | collective-permute-done | bytes 524320 | tf_op jit(solution)/shard_map/ppermute | solution.py:35
  128.6 3.2 %collective-permute-start.31 = (bf16[16,128,128]{2,1,0:T(8,128)(2,1)S(1)}, bf16[16,128,128]{2,1,0:T(8,128)(2,1)S(1)}, u32[]{:S(2)}, u32[]{:S(2)}) collective-permute-start(bf16[16,128,128]{2,1,0:T(8,128)(2,1)S(1)} %add_convert_fusion.1), channel_id=1, source_target_pairs={{0,196},{1,197},{2,198},{3,199},{8,204},{9,205},{10,206},{11,207},... | collective-permute-start | bytes 1572872 | tf_op jit(solution)/shard_map/ppermute | solution.py:35
  132.3 1.6 %collective-permute-start.27 = (bf16[2,4,8192]{2,1,0:T(4,128)(2,1)S(1)}, bf16[2,4,8192]{2,1,0:T(4,128)(2,1)S(1)}, u32[]{:S(2)}, u32[]{:S(2)}) collective-permute-start(bf16[2,4,8192]{2,1,0:T(4,128)(2,1)S(1)} %get-tuple-element.78), channel_id=1, source_target_pairs={{0,1},{1,2},{2,3},{3,0},{8,9},{9,10},{10,11},{11,8},{16,17},{17,18... | collective-permute-start | bytes 393224 | tf_op jit(solution)/shard_map/ppermute | solution.py:35
  133.9 1.5 %collective-permute-start.28 = (bf16[2,4,8192]{2,1,0:T(4,128)(2,1)S(1)}, bf16[2,4,8192]{2,1,0:T(4,128)(2,1)S(1)}, u32[]{:S(2)}, u32[]{:S(2)}) collective-permute-start(bf16[2,4,8192]{2,1,0:T(4,128)(2,1)S(1)} %get-tuple-element.77), channel_id=1, source_target_pairs={{0,2},{1,3},{2,0},{3,1},{8,10},{9,11},{10,8},{11,9},{16,18},{17,19... | collective-permute-start | bytes 393224 | tf_op jit(solution)/shard_map/ppermute | solution.py:35
  135.3 1.8 %collective-permute-start.29 = (bf16[2,4,8192]{2,1,0:T(4,128)(2,1)S(1)}, bf16[2,4,8192]{2,1,0:T(4,128)(2,1)S(1)}, u32[]{:S(2)}, u32[]{:S(2)}) collective-permute-start(bf16[2,4,8192]{2,1,0:T(4,128)(2,1)S(1)} %get-tuple-element.76), channel_id=1, source_target_pairs={{0,3},{1,0},{2,1},{3,2},{8,11},{9,8},{10,9},{11,10},{16,19},{17,16... | collective-permute-start | bytes 393224 | tf_op jit(solution)/shard_map/ppermute | solution.py:35
  137.1 3.6 %collective-permute-done.30 = bf16[16,128,128]{2,1,0:T(8,128)(2,1)S(1)} collective-permute-done((bf16[16,128,128]{2,1,0:T(8,128)(2,1)S(1)}, bf16[16,128,128]{2,1,0:T(8,128)(2,1)S(1)}, u32[]{:S(2)}, u32[]{:S(2)}) %collective-permute-start.30) | collective-permute-done | bytes 524320 | tf_op jit(solution)/shard_map/ppermute | solution.py:35
  (108 shorter events, 21.9 us)
Async XLA Ops:
  1.9 8.8 %collective-permute-start.4 = (bf16[2,2,2,128,128]{4,3,1,0,2:T(8,128)(2,1)S(1)}, bf16[2,2,2,128,128]{4,3,1,0,2:T(8,128)(2,1)S(1)}, u32[]{:S(2)}, u32[]{:S(2)}) collective-permute-start(bf16[2,2,2,128,128]{4,3,1,0,2:T(8,128)(2,1)S(1)} %get-tuple-element.81), channel_id=1, source_target_pairs={{0,32},{1,33},{2,34},{3,35},{8,40},{9,41},{10,42},{11,43},{16,48},... | collective-permute-start | bytes 786440 | tf_op jit(solution)/shard_map/ppermute | solution.py:35
  3.5 12.6 %collective-permute-start = (s32[4,17]{1,0:T(4,128)S(1)}, s32[4,17]{1,0:T(4,128)S(1)}, u32[]{:S(2)}, u32[]{:S(2)}) collective-permute-start(s32[4,17]{1,0:T(4,128)S(1)} %pad_add_fusion), channel_id=1, source_target_pairs={{0,4},{1,5},{2,6},{3,7},{8,12},{9,13},{10,14},{11,15},{16,20},{17,... | collective-permute-start | bytes 824 | tf_op jit(solution)/shard_map/ppermute | solution.py:35
  10.8 14.1 %collective-permute-start.5 = (bf16[16,128,128]{2,1,0:T(8,128)(2,1)S(1)}, bf16[16,128,128]{2,1,0:T(8,128)(2,1)S(1)}, u32[]{:S(2)}, u32[]{:S(2)}) collective-permute-start(bf16[16,128,128]{2,1,0:T(8,128)(2,1)S(1)} %bitcast.30), channel_id=1, source_target_pairs={{0,196},{1,197},{2,198},{3,199},{8,204},{9,205},{10,206},{11,207},... | collective-permute-start | bytes 1572872 | tf_op jit(solution)/shard_map/ppermute | solution.py:35
  11.0 15.2 %collective-permute-start.6 = (bf16[16,128,128]{2,1,0:T(8,128)(2,1)S(1)}, bf16[16,128,128]{2,1,0:T(8,128)(2,1)S(1)}, u32[]{:S(2)}, u32[]{:S(2)}) collective-permute-start(bf16[16,128,128]{2,1,0:T(8,128)(2,1)S(1)} %bitcast.31), channel_id=1, source_target_pairs={{0,64},{1,65},{2,66},{3,67},{8,72},{9,73},{10,74},{11,75},{16,80},... | collective-permute-start | bytes 1572872 | tf_op jit(solution)/shard_map/ppermute | solution.py:35
  13.0 5.6 %collective-permute-start.1 = (bf16[2,4,8192]{2,1,0:T(4,128)(2,1)S(1)}, bf16[2,4,8192]{2,1,0:T(4,128)(2,1)S(1)}, u32[]{:S(2)}, u32[]{:S(2)}) collective-permute-start(bf16[2,4,8192]{2,1,0:T(4,128)(2,1)S(1)} %pad_maximum_fusion.1), channel_id=1, source_target_pairs={{0,3},{1,0},{2,1},{3,2},{8,11},{9,8},{10,9},{11,10},{16,19},{17,16... | collective-permute-start | bytes 393224 | tf_op jit(solution)/shard_map/ppermute | solution.py:35
  13.6 8.3 %collective-permute-start.2 = (bf16[2,4,8192]{2,1,0:T(4,128)(2,1)S(1)}, bf16[2,4,8192]{2,1,0:T(4,128)(2,1)S(1)}, u32[]{:S(2)}, u32[]{:S(2)}) collective-permute-start(bf16[2,4,8192]{2,1,0:T(4,128)(2,1)S(1)} %pad_maximum_fusion.1), channel_id=1, source_target_pairs={{0,2},{1,3},{2,0},{3,1},{8,10},{9,11},{10,8},{11,9},{16,18},{17,19... | collective-permute-start | bytes 393224 | tf_op jit(solution)/shard_map/ppermute | solution.py:35
  16.0 6.7 %collective-permute-start.3 = (bf16[2,4,8192]{2,1,0:T(4,128)(2,1)S(1)}, bf16[2,4,8192]{2,1,0:T(4,128)(2,1)S(1)}, u32[]{:S(2)}, u32[]{:S(2)}) collective-permute-start(bf16[2,4,8192]{2,1,0:T(4,128)(2,1)S(1)} %pad_maximum_fusion.1), channel_id=1, source_target_pairs={{0,1},{1,2},{2,3},{3,0},{8,9},{9,10},{10,11},{11,8},{16,17},{17,18... | collective-permute-start | bytes 393224 | tf_op jit(solution)/shard_map/ppermute | solution.py:35
  26.2 13.2 %collective-permute-start.10 = (bf16[16,128,128]{2,1,0:T(8,128)(2,1)S(1)}, bf16[16,128,128]{2,1,0:T(8,128)(2,1)S(1)}, u32[]{:S(2)}, u32[]{:S(2)}) collective-permute-start(bf16[16,128,128]{2,1,0:T(8,128)(2,1)S(1)} %collective-permute-done.5.refs_6_), channel_id=1, source_target_pairs={{0,196},{1,197},{2,198},{3,199},{8,204},{9,205},{10,206},{11,207},... | collective-permute-start | bytes 1572872 | tf_op jit(solution)/shard_map/ppermute | solution.py:35
  26.6 14.7 %collective-permute-start.12 = (bf16[16,128,128]{2,1,0:T(8,128)(2,1)S(1)}, bf16[16,128,128]{2,1,0:T(8,128)(2,1)S(1)}, u32[]{:S(2)}, u32[]{:S(2)}) collective-permute-start(bf16[16,128,128]{2,1,0:T(8,128)(2,1)S(1)} %collective-permute-done.6.refs_9_), channel_id=1, source_target_pairs={{0,64},{1,65},{2,66},{3,67},{8,72},{9,73},{10,74},{11,75},{16,80},... | collective-permute-start | bytes 1572872 | tf_op jit(solution)/shard_map/ppermute | solution.py:35
  28.6 24.5 %collective-permute-start.7 = (bf16[2,16,8192]{2,1,0:T(8,128)(2,1)S(1)}, bf16[2,16,8192]{2,1,0:T(8,128)(2,1)S(1)}, u32[]{:S(2)}, u32[]{:S(2)}) collective-permute-start(bf16[2,16,8192]{2,1,0:T(8,128)(2,1)S(1)} %pad_maximum_fusion), channel_id=1, source_target_pairs={{0,24},{1,25},{2,26},{3,27},{8,0},{9,1},{10,2},{11,3},{16,8},{17,9... | collective-permute-start | bytes 1572872 | tf_op jit(solution)/shard_map/ppermute | solution.py:35
  31.6 21.4 %collective-permute-start.8 = (bf16[2,16,8192]{2,1,0:T(8,128)(2,1)S(1)}, bf16[2,16,8192]{2,1,0:T(8,128)(2,1)S(1)}, u32[]{:S(2)}, u32[]{:S(2)}) collective-permute-start(bf16[2,16,8192]{2,1,0:T(8,128)(2,1)S(1)} %pad_maximum_fusion), channel_id=1, source_target_pairs={{0,16},{1,17},{2,18},{3,19},{8,24},{9,25},{10,26},{11,27},{16,0},{... | collective-permute-start | bytes 1572872 | tf_op jit(solution)/shard_map/ppermute | solution.py:35
  32.3 24.5 %collective-permute-start.9 = (bf16[2,16,8192]{2,1,0:T(8,128)(2,1)S(1)}, bf16[2,16,8192]{2,1,0:T(8,128)(2,1)S(1)}, u32[]{:S(2)}, u32[]{:S(2)}) collective-permute-start(bf16[2,16,8192]{2,1,0:T(8,128)(2,1)S(1)} %pad_maximum_fusion), channel_id=1, source_target_pairs={{0,8},{1,9},{2,10},{3,11},{8,16},{9,17},{10,18},{11,19},{16,24},{1... | collective-permute-start | bytes 1572872 | tf_op jit(solution)/shard_map/ppermute | solution.py:35
  39.4 17.3 %collective-permute-start.11 = (bf16[16,128,128]{2,1,0:T(8,128)(2,1)S(1)}, bf16[16,128,128]{2,1,0:T(8,128)(2,1)S(1)}, u32[]{:S(2)}, u32[]{:S(2)}) collective-permute-start(bf16[16,128,128]{2,1,0:T(8,128)(2,1)S(1)} %collective-permute-done.10.refs_7_), channel_id=1, source_target_pairs={{0,196},{1,197},{2,198},{3,199},{8,204},{9,205},{10,206},{11,207},... | collective-permute-start | bytes 1572872 | tf_op jit(solution)/shard_map/ppermute | solution.py:35
  41.2 15.5 %collective-permute-start.13 = (bf16[16,128,128]{2,1,0:T(8,128)(2,1)S(1)}, bf16[16,128,128]{2,1,0:T(8,128)(2,1)S(1)}, u32[]{:S(2)}, u32[]{:S(2)}) collective-permute-start(bf16[16,128,128]{2,1,0:T(8,128)(2,1)S(1)} %collective-permute-done.12.refs_10_), channel_id=1, source_target_pairs={{0,64},{1,65},{2,66},{3,67},{8,72},{9,73},{10,74},{11,75},{16,80},... | collective-permute-start | bytes 1572872 | tf_op jit(solution)/shard_map/ppermute | solution.py:35
  57.0 12.0 %collective-permute-start.14 = (bf16[2,64,8192]{2,1,0:T(8,128)(2,1)S(1)}, bf16[2,64,8192]{2,1,0:T(8,128)(2,1)}, u32[]{:S(2)}, u32[]{:S(2)}) collective-permute-start(bf16[2,64,8192]{2,1,0:T(8,128)(2,1)S(1)} %constant_dynamic-update-slice_fusion.refs_3_), channel_id=1, source_target_pairs={{0,32},{1,33},{2,34},{3,35},{8,40},{9,41},{10,42},{11,43},{16,48},... | collective-permute-start | bytes 6291464 | tf_op jit(solution)/shard_map/ppermute | solution.py:35
  57.6 8.3 %collective-permute-start.15 = (bf16[8,128,128]{2,1,0:T(8,128)(2,1)S(1)}, bf16[8,128,128]{2,1,0:T(8,128)(2,1)S(1)}, u32[]{:S(2)}, u32[]{:S(2)}) collective-permute-start(bf16[8,128,128]{2,1,0:T(8,128)(2,1)S(1)} %slice.80), channel_id=1, source_target_pairs={{0,196},{1,197},{2,198},{3,199},{8,204},{9,205},{10,206},{11,207},... | collective-permute-start | bytes 786440 | tf_op jit(solution)/shard_map/ppermute | solution.py:35
  59.5 9.4 %collective-permute-start.16 = (bf16[8,128,128]{2,1,0:T(8,128)(2,1)S(1)}, bf16[8,128,128]{2,1,0:T(8,128)(2,1)S(1)}, u32[]{:S(2)}, u32[]{:S(2)}) collective-permute-start(bf16[8,128,128]{2,1,0:T(8,128)(2,1)S(1)} %slice.81), channel_id=1, source_target_pairs={{0,64},{1,65},{2,66},{3,67},{8,72},{9,73},{10,74},{11,75},{16,80},... | collective-permute-start | bytes 786440 | tf_op jit(solution)/shard_map/ppermute | solution.py:35
  82.8 13.5 %collective-permute-start.17 = (bf16[2,64,8192]{2,1,0:T(8,128)(2,1)}, bf16[2,64,8192]{2,1,0:T(8,128)(2,1)S(1)}, u32[]{:S(2)}, u32[]{:S(2)}) collective-permute-start(bf16[2,64,8192]{2,1,0:T(8,128)(2,1)} %get-tuple-element.45), channel_id=1, source_target_pairs={{0,32},{1,33},{2,34},{3,35},{8,40},{9,41},{10,42},{11,43},{16,48},... | collective-permute-start | bytes 6291464 | tf_op jit(solution)/shard_map/ppermute | solution.py:35
  82.9 8.9 %collective-permute-start.23 = (bf16[8,128,128]{2,1,0:T(8,128)(2,1)}, bf16[8,128,128]{2,1,0:T(8,128)(2,1)S(1)}, u32[]{:S(2)}, u32[]{:S(2)}) collective-permute-start(bf16[8,128,128]{2,1,0:T(8,128)(2,1)} %get-tuple-element.52), channel_id=1, source_target_pairs={{0,196},{1,197},{2,198},{3,199},{8,204},{9,205},{10,206},{11,207},... | collective-permute-start | bytes 786440 | tf_op jit(solution)/shard_map/ppermute | solution.py:35
  83.0 11.5 %collective-permute-start.21 = (bf16[8,128,128]{2,1,0:T(8,128)(2,1)}, bf16[8,128,128]{2,1,0:T(8,128)(2,1)S(1)}, u32[]{:S(2)}, u32[]{:S(2)}) collective-permute-start(bf16[8,128,128]{2,1,0:T(8,128)(2,1)} %get-tuple-element.49), channel_id=1, source_target_pairs={{0,64},{1,65},{2,66},{3,67},{8,72},{9,73},{10,74},{11,75},{16,80},... | collective-permute-start | bytes 786440 | tf_op jit(solution)/shard_map/ppermute | solution.py:35
  93.0 13.6 %collective-permute-start.24 = (bf16[16,128,128]{2,1,0:T(8,128)(2,1)S(1)}, bf16[16,128,128]{2,1,0:T(8,128)(2,1)S(1)}, u32[]{:S(2)}, u32[]{:S(2)}) collective-permute-start(bf16[16,128,128]{2,1,0:T(8,128)(2,1)S(1)} %add_convert_fusion.5), channel_id=1, source_target_pairs={{0,196},{1,197},{2,198},{3,199},{8,204},{9,205},{10,206},{11,207},... | collective-permute-start | bytes 1572872 | tf_op jit(solution)/shard_map/ppermute | solution.py:35
  95.7 14.7 %collective-permute-start.22 = (bf16[16,128,128]{2,1,0:T(8,128)(2,1)S(1)}, bf16[16,128,128]{2,1,0:T(8,128)(2,1)S(1)}, u32[]{:S(2)}, u32[]{:S(2)}) collective-permute-start(bf16[16,128,128]{2,1,0:T(8,128)(2,1)S(1)} %add_convert_fusion.7), channel_id=1, source_target_pairs={{0,64},{1,65},{2,66},{3,67},{8,72},{9,73},{10,74},{11,75},{16,80},... | collective-permute-start | bytes 1572872 | tf_op jit(solution)/shard_map/ppermute | solution.py:35
  96.8 14.5 %collective-permute-start.18 = (bf16[2,16,8192]{2,1,0:T(8,128)(2,1)S(1)}, bf16[2,16,8192]{2,1,0:T(8,128)(2,1)S(1)}, u32[]{:S(2)}, u32[]{:S(2)}) collective-permute-start(bf16[2,16,8192]{2,1,0:T(8,128)(2,1)S(1)} %get-tuple-element.70), channel_id=1, source_target_pairs={{0,8},{1,9},{2,10},{3,11},{8,16},{9,17},{10,18},{11,19},{16,24},{1... | collective-permute-start | bytes 1572872 | tf_op jit(solution)/shard_map/ppermute | solution.py:35
  96.9 14.4 %collective-permute-start.19 = (bf16[2,16,8192]{2,1,0:T(8,128)(2,1)S(1)}, bf16[2,16,8192]{2,1,0:T(8,128)(2,1)S(1)}, u32[]{:S(2)}, u32[]{:S(2)}) collective-permute-start(bf16[2,16,8192]{2,1,0:T(8,128)(2,1)S(1)} %get-tuple-element.69), channel_id=1, source_target_pairs={{0,24},{1,25},{2,26},{3,27},{8,0},{9,1},{10,2},{11,3},{16,8},{17,9... | collective-permute-start | bytes 1572872 | tf_op jit(solution)/shard_map/ppermute | solution.py:35
  111.3 12.8 %collective-permute-start.26 = (bf16[16,128,128]{2,1,0:T(8,128)(2,1)}, bf16[16,128,128]{2,1,0:T(8,128)(2,1)}, u32[]{:S(2)}, u32[]{:S(2)}) collective-permute-start(bf16[16,128,128]{2,1,0:T(8,128)(2,1)} %add_convert_fusion.4), channel_id=1, source_target_pairs={{0,196},{1,197},{2,198},{3,199},{8,204},{9,205},{10,206},{11,207},... | collective-permute-start | bytes 1572872 | tf_op jit(solution)/shard_map/ppermute | solution.py:35
  113.9 13.4 %collective-permute-start.25 = (bf16[16,128,128]{2,1,0:T(8,128)(2,1)}, bf16[16,128,128]{2,1,0:T(8,128)(2,1)}, u32[]{:S(2)}, u32[]{:S(2)}) collective-permute-start(bf16[16,128,128]{2,1,0:T(8,128)(2,1)} %add_convert_fusion.6), channel_id=1, source_target_pairs={{0,64},{1,65},{2,66},{3,67},{8,72},{9,73},{10,74},{11,75},{16,80},... | collective-permute-start | bytes 1572872 | tf_op jit(solution)/shard_map/ppermute | solution.py:35
  113.9 14.6 %collective-permute-start.20 = (bf16[2,16,8192]{2,1,0:T(8,128)(2,1)S(1)}, bf16[2,16,8192]{2,1,0:T(8,128)(2,1)S(1)}, u32[]{:S(2)}, u32[]{:S(2)}) collective-permute-start(bf16[2,16,8192]{2,1,0:T(8,128)(2,1)S(1)} %get-tuple-element.46), channel_id=1, source_target_pairs={{0,16},{1,17},{2,18},{3,19},{8,24},{9,25},{10,26},{11,27},{16,0},{... | collective-permute-start | bytes 1572872 | tf_op jit(solution)/shard_map/ppermute | solution.py:35
  128.5 12.3 %collective-permute-start.30 = (bf16[16,128,128]{2,1,0:T(8,128)(2,1)S(1)}, bf16[16,128,128]{2,1,0:T(8,128)(2,1)S(1)}, u32[]{:S(2)}, u32[]{:S(2)}) collective-permute-start(bf16[16,128,128]{2,1,0:T(8,128)(2,1)S(1)} %add_convert_fusion.2), channel_id=1, source_target_pairs={{0,64},{1,65},{2,66},{3,67},{8,72},{9,73},{10,74},{11,75},{16,80},... | collective-permute-start | bytes 1572872 | tf_op jit(solution)/shard_map/ppermute | solution.py:35
  128.6 12.2 %collective-permute-start.31 = (bf16[16,128,128]{2,1,0:T(8,128)(2,1)S(1)}, bf16[16,128,128]{2,1,0:T(8,128)(2,1)S(1)}, u32[]{:S(2)}, u32[]{:S(2)}) collective-permute-start(bf16[16,128,128]{2,1,0:T(8,128)(2,1)S(1)} %add_convert_fusion.1), channel_id=1, source_target_pairs={{0,196},{1,197},{2,198},{3,199},{8,204},{9,205},{10,206},{11,207},... | collective-permute-start | bytes 1572872 | tf_op jit(solution)/shard_map/ppermute | solution.py:35
  132.3 8.9 %collective-permute-start.27 = (bf16[2,4,8192]{2,1,0:T(4,128)(2,1)S(1)}, bf16[2,4,8192]{2,1,0:T(4,128)(2,1)S(1)}, u32[]{:S(2)}, u32[]{:S(2)}) collective-permute-start(bf16[2,4,8192]{2,1,0:T(4,128)(2,1)S(1)} %get-tuple-element.78), channel_id=1, source_target_pairs={{0,1},{1,2},{2,3},{3,0},{8,9},{9,10},{10,11},{11,8},{16,17},{17,18... | collective-permute-start | bytes 393224 | tf_op jit(solution)/shard_map/ppermute | solution.py:35
  133.9 7.3 %collective-permute-start.28 = (bf16[2,4,8192]{2,1,0:T(4,128)(2,1)S(1)}, bf16[2,4,8192]{2,1,0:T(4,128)(2,1)S(1)}, u32[]{:S(2)}, u32[]{:S(2)}) collective-permute-start(bf16[2,4,8192]{2,1,0:T(4,128)(2,1)S(1)} %get-tuple-element.77), channel_id=1, source_target_pairs={{0,2},{1,3},{2,0},{3,1},{8,10},{9,11},{10,8},{11,9},{16,18},{17,19... | collective-permute-start | bytes 393224 | tf_op jit(solution)/shard_map/ppermute | solution.py:35
  135.3 6.4 %collective-permute-start.29 = (bf16[2,4,8192]{2,1,0:T(4,128)(2,1)S(1)}, bf16[2,4,8192]{2,1,0:T(4,128)(2,1)S(1)}, u32[]{:S(2)}, u32[]{:S(2)}) collective-permute-start(bf16[2,4,8192]{2,1,0:T(4,128)(2,1)S(1)} %get-tuple-element.76), channel_id=1, source_target_pairs={{0,3},{1,0},{2,1},{3,2},{8,11},{9,8},{10,9},{11,10},{16,19},{17,16... | collective-permute-start | bytes 393224 | tf_op jit(solution)/shard_map/ppermute | solution.py:35
  (21 other events, 282.2 us)
where the time goes:
time: 145 us; the launch traced here: 144 us
  waiting for transfers between devices  69 us (48%)
  starting transfers between devices  45.5 us (31%)
  Pallas kernels  13.1 us (9%)
  other arithmetic  10.2 us (7%)
  local copies, waits for them, and re-layouts  4.7 us (3%)
    ppermute x33, waiting for transfers between devices, send(): return lax.ppermute(value, ('row', 'col'), pairs)  69 us
    ppermute x33, starting transfers between devices, send(): return lax.ppermute(value, ('row', 'col'), pairs)  45.5 us
    pallas_call x1, Pallas kernels, products(): pl.pallas_call(functools.partial(products_kernel, slots), out_shape=[jax....  13.1 us
  transfers between devices with their start and end apart: 33, of which 18 were waited for; matrix products, arithmetic and copies ran while one was open for 8% of the time, Pallas kernels for 0%

commit v1 on v0

--- a/solution.py
+++ b/solution.py
@@ -15,6 +15,7 @@
 NT = (((1,), (1,)), ((), ()))
 TN = (((0,), (0,)), ((), ()))
 HOPS = (0, 1, 2, 3, -1, -2, -3, 4)
+LIST_ROWS = 16
 
 
 def device(z, core, y, x):
@@ -54,7 +55,7 @@
     place, index, count = refs[:3]
     rows_in, weights_in = refs[3:5], refs[5:14]
     grads_out, sums_out = refs[14:23], refs[23:25]
-    act, cot, weights, grads, out_sum, in_sum, sums, a_cat, c_cat, up_cat, down_cat = refs[25:36]
+    act, cot, weights, grads, out_sum, in_sum, sums, *cats = refs[25:36]
     row_sems, weight_sems, grad_sems, sum_sems = refs[36:]
     rows = act.shape[0]
     half = rows // 2
@@ -68,15 +69,20 @@
         arrivals.append(pltpu.make_async_copy(rows_in[o].at[1], cot.at[span], row_sems.at[2 + o]))
     for copy in arrivals:
         copy.start()
+    size = weights.shape[1]
     near, loads, stores = [], [], []
     for n, hop in enumerate(hops):
         there = (z + hop + NZ) % NZ
-        spots = weights.at[there], grads.at[there]
+        near.append(there // NL == own)
         if hop == 4:
-            spots = [spot.at[pl.ds(8 * (n - 7), 8)] for spot in spots]
-        near.append(there // NL == own)
-        loads.append(pltpu.make_async_copy(weights_in[n], spots[0], weight_sems.at[n]))
-        stores.append(pltpu.make_async_copy(spots[1], grads_out[n], grad_sems.at[n]))
+            first = n - 7
+            source, spot = weights_in[n], weights.at[there, pl.ds(first * (size // 2), size // 2)]
+            result = grads.at[there, pl.ds(8 * first, 8)]
+        else:
+            source, spot = weights_in[n].at[pl.ds(0, size)], weights.at[there]
+            result = grads.at[there]
+        loads.append(pltpu.make_async_copy(source, spot, weight_sems.at[n]))
+        stores.append(pltpu.make_async_copy(result, grads_out[n], grad_sems.at[n]))
     for n in range(9):
         pl.when(near[n])(loads[n].start)
     for n in range(9):
@@ -92,6 +98,7 @@
         far, p = n // 2, n % 2
         base = (1 - own if far else own) * NL
         live = count[n]
+        a_cat, c_cat, up_cat, down_cat = [cat.at[n % 2] for cat in cats]
         if n == 2:
             for m in range(9):
                 pl.when(jnp.logical_not(near[m]))(loads[m].wait)
@@ -101,8 +108,9 @@
             here = slice(k * BLK, (k + 1) * BLK)
             a_cat[:, here] = act[:, lanes]
             c_cat[:, here] = cot[:, lanes]
-            up = weights[base + k // 4, k % 4 * 4 + p * 2]
-            down = weights[base + k // 4, k % 4 * 4 + p * 2 + 1]
+            spot = (k % 4 * 4 + p * 2) * BLK
+            up = weights[base + k // 4, spot : spot + BLK]
+            down = weights[base + k // 4, spot + BLK : spot + 2 * BLK]
             up_cat[here, :] = jnp.where(k < live, up, jnp.zeros_like(up))
             down_cat[:, here] = jnp.where(k < live, down, jnp.zeros_like(down))
         preact = jnp.dot(a_cat[...], up_cat[...], preferred_element_type=F32)
@@ -141,11 +149,12 @@
 def products(place, index, count, row_pair, weights):
     panels, slots = index.shape
     _, half, features = row_pair[0].shape
-    shard = weights[0].shape
+    size = 2 * weights[7].shape[0]
+    blocks = size // BLK
     rows, wide = 2 * half, slots * BLK
     any_space = pl.BlockSpec(memory_space=pl.ANY)
     smem = pl.BlockSpec(memory_space=pltpu.SMEM)
-    shapes = [part.shape for part in weights] + [(2, half, features)] * 2
+    shapes = [(blocks, BLK, BLK)] * 7 + [(blocks // 2, BLK, BLK)] * 2 + [(2, half, features)] * 2
     results = pl.pallas_call(
         functools.partial(products_kernel, slots),
         out_shape=[jax.ShapeDtypeStruct(shape, BF) for shape in shapes],
@@ -154,15 +163,15 @@
         scratch_shapes=[
             pltpu.VMEM((rows, features), BF),
             pltpu.VMEM((rows, features), BF),
-            pltpu.VMEM((NZ,) + shard, BF),
-            pltpu.VMEM((NZ,) + shard, BF),
+            pltpu.VMEM((NZ, size, BLK), BF),
+            pltpu.VMEM((NZ, blocks, BLK, BLK), BF),
             pltpu.VMEM((rows, features), F32),
             pltpu.VMEM((rows, features), F32),
             pltpu.VMEM((2, 2, half, features), BF),
-            pltpu.VMEM((rows, wide), BF),
-            pltpu.VMEM((rows, wide), BF),
-            pltpu.VMEM((wide, BLK), BF),
-            pltpu.VMEM((BLK, wide), BF),
+            pltpu.VMEM((2, rows, wide), BF),
+            pltpu.VMEM((2, rows, wide), BF),
+            pltpu.VMEM((2, wide, BLK), BF),
+            pltpu.VMEM((2, BLK, wide), BF),
             pltpu.SemaphoreType.DMA((4,)),
             pltpu.SemaphoreType.DMA((9,)),
             pltpu.SemaphoreType.DMA((9,)),
@@ -174,16 +183,6 @@
     return results[:9], results[9:]
 
 
-def ring_gather(shard):
-    up, down = [shard], [shard]
-    for _ in range(3):
-        up.append(send(up[-1], dz=-1))
-        down.append(send(down[-1], dz=1))
-    half = shard.shape[0] // 2
-    across = [send(up[-1][:half], dz=-1), send(down[-1][half:], dz=1)]
-    return [shard] + up[1:] + down[1:] + across
-
-
 def pair(up, down):
     return send(up, dz=1), send(down, dz=-1)
 
@@ -204,24 +203,36 @@
     core, low, high = row % NC, row // NC, (col // NX) % NH
     own_first = core == 0
 
-    lists = jnp.concatenate([block_index, block_count[:, None]], axis=1)
-    far_lists = send(lists, dz=4)
-    lists = lax.dynamic_slice_in_dim(jnp.stack([lists, far_lists]), 2 * core, 2, axis=1).reshape(4, -1)
-    index, count = lists[:, :-1], lists[:, -1]
     place = (high * NL + low).astype(jnp.int32).reshape(1)
 
     both = jnp.stack([up_panels, down_panels], axis=2)
     keep = lax.dynamic_slice_in_dim(both, 2 * core, 2, axis=1)
     got = swap_cores(lax.dynamic_slice_in_dim(both, 2 - 2 * core, 2, axis=1))
-    shard = jnp.where(own_first, jnp.stack([keep, got]), jnp.stack([got, keep]))
-    weights = ring_gather(shard.reshape(-1, BLK, BLK))
-
+    shard = jnp.where(own_first, jnp.stack([keep, got]), jnp.stack([got, keep])).reshape(-1, BLK)
+    lists = jnp.concatenate([block_index, block_count[:, None]], axis=1)
+    row_of_lists = lists.reshape(1, -1).astype(BF)
+    row_of_lists = jnp.pad(row_of_lists, ((0, LIST_ROWS - 1), (0, BLK - row_of_lists.shape[1])))
+    shard = jnp.concatenate([shard, row_of_lists])
+    ring_1 = send(shard, dz=-1), send(shard, dz=1)
     rows = jnp.stack([activations, cotangent])
     rows = [rows] + [send(rows, dx=-d) for d in (1, 2, 3)]
-    rows = jnp.concatenate(after(rows, far_lists, weights[1], weights[4]), axis=1)
-    rows = after([rows] + [send(rows, dy=-d) for d in (1, 2, 3)], weights[3], weights[6])
+    rows = jnp.concatenate(after(rows, *ring_1), axis=1)
+    up, down = after(ring_1, rows)
+    ring_2 = send(up, dz=-1), send(down, dz=1)
+    size = shard.shape[0] - LIST_ROWS
+    ring_3 = send(ring_2[0][:size], dz=-1), send(ring_2[1][:size], dz=1)
+    ring_4 = send(ring_3[0][: size // 2], dz=-1), send(ring_3[1][size // 2 :], dz=1)
+    weights = [shard, ring_1[0], ring_2[0], ring_3[0], ring_1[1], ring_2[1], ring_3[1], *ring_4]
+    rows = after([rows] + [send(rows, dy=-d) for d in (1, 2, 3)], *ring_3)
     rows = jnp.concatenate(rows, axis=1)
     row_pair = [rows, swap_cores(rows)]
+
+    below, above = [v[1][-LIST_ROWS] for v in (ring_1, ring_2)], [v[0][-LIST_ROWS] for v in (ring_2, ring_1)]
+    far_lists = jnp.where(low < 2, jnp.where(low == 0, *below), jnp.where(low == 2, *above))
+    far_lists = far_lists[: lists.size]
+    far_lists = far_lists.astype(jnp.int32).reshape(lists.shape)
+    lists = lax.dynamic_slice_in_dim(jnp.stack([lists, far_lists]), 2 * core, 2, axis=1).reshape(4, -1)
+    index, count = lists[:, :-1], lists[:, -1]
 
     parts, (own, far) = products(place, index, count, row_pair, weights)
     step_1 = pair(parts[7], parts[8])

time: 145 us -> 145 us (level)
  waiting for transfers between devices: 69 us -> 66.5 us
  local copies, waits for them, and re-layouts: 4.7 us -> 6.32 us
    ppermute x33 -> x32, waiting for transfers between devices: 69 us -> 66.5 us  [send(): return lax.ppermute(value, ('row', 'col'), pairs)]
    slice x2 -> x4, local copies, waits for them, and re-layouts: 0.04 us -> 2 us  [the longest x1 0.97 us: shards(): ring_3[0][:size // 2]]
    ppermute x33 -> x32, starting transfers between devices: 45.5 us -> 45.9 us  [send(): return lax.ppermute(value, ('row', 'col'), pairs)]
  transfers between devices with their start and end apart: 33 -> 32, of which waited for: 18 -> 17; matrix products, arithmetic and copies ran while one was open for 8% -> 10% of each run, Pallas kernels for 0% -> 0%
where the time goes in v1:
time: 145 us; the launch traced here: 143 us
  waiting for transfers between devices  66.5 us (46%)
  starting transfers between devices  45.9 us (32%)
  Pallas kernels  12.5 us (9%)
  other arithmetic  10.9 us (8%)
  local copies, waits for them, and re-layouts  6.32 us (4%)
    ppermute x32, waiting for transfers between devices, send(): return lax.ppermute(value, ('row', 'col'), pairs)  66.5 us
    ppermute x32, starting transfers between devices, send(): return lax.ppermute(value, ('row', 'col'), pairs)  45.9 us
    pallas_call x1, Pallas kernels, products(): pl.pallas_call(functools.partial(products_kernel, slots), out_shape=[jax....  12.5 us
  transfers between devices with their start and end apart: 32, of which 17 were waited for; matrix products, arithmetic and copies ran while one was open for 10% of the time, Pallas kernels for 0%

profile of v1, /device:TPU:2, one launch (start us, length us, event | category | flops | bytes accessed | tf_op | source)
XLA Modules:
  0.0 143.2 jit_solution(17818019513356187661)
XLA Ops:
  3.7 2.0 %collective-permute-start.1 = (bf16[2064,128]{1,0:T(8,128)(2,1)S(1)}, bf16[2064,128]{1,0:T(8,128)(2,1)S(1)}, u32[]{:S(2)}, u32[]{:S(2)}) collective-permute-start(bf16[2064,128]{1,0:T(8,128)(2,1)S(1)} %fusion.1.refs_5_), channel_id=1, source_target_pairs={{0,64},{1,65},{2,66},{3,67},{8,72},{9,73},{10,74},{11,75},{16,80},... | collective-permute-start | bytes 1585160 | tf_op jit(solution)/shard_map/ppermute | solution.py:36
  5.7 4.0 %collective-permute-start.2 = (bf16[2064,128]{1,0:T(8,128)(2,1)S(1)}, bf16[2064,128]{1,0:T(8,128)(2,1)S(1)}, u32[]{:S(2)}, u32[]{:S(2)}) collective-permute-start(bf16[2064,128]{1,0:T(8,128)(2,1)S(1)} %fusion.1.refs_5_), channel_id=1, source_target_pairs={{0,196},{1,197},{2,198},{3,199},{8,204},{9,205},{10,206},{11,207},... | collective-permute-start | bytes 1585160 | tf_op jit(solution)/shard_map/ppermute | solution.py:36
  10.5 2.4 %collective-permute-start.4 = (bf16[2,4,8192]{2,1,0:T(4,128)(2,1)S(1)}, bf16[2,4,8192]{2,1,0:T(4,128)(2,1)S(1)}, u32[]{:S(2)}, u32[]{:S(2)}) collective-permute-start(bf16[2,4,8192]{2,1,0:T(4,128)(2,1)S(1)} %pad_maximum_fusion.1), channel_id=1, source_target_pairs={{0,2},{1,3},{2,0},{3,1},{8,10},{9,11},{10,8},{11,9},{16,18},{17,19... | collective-permute-start | bytes 393224 | tf_op jit(solution)/shard_map/ppermute | solution.py:36
  12.9 1.8 %collective-permute-start.5 = (bf16[2,4,8192]{2,1,0:T(4,128)(2,1)S(1)}, bf16[2,4,8192]{2,1,0:T(4,128)(2,1)S(1)}, u32[]{:S(2)}, u32[]{:S(2)}) collective-permute-start(bf16[2,4,8192]{2,1,0:T(4,128)(2,1)S(1)} %pad_maximum_fusion.1), channel_id=1, source_target_pairs={{0,1},{1,2},{2,3},{3,0},{8,9},{9,10},{10,11},{11,8},{16,17},{17,18... | collective-permute-start | bytes 393224 | tf_op jit(solution)/shard_map/ppermute | solution.py:36
  15.6 3.7 %collective-permute-done.4 = bf16[2,4,8192]{2,1,0:T(4,128)(2,1)S(1)} collective-permute-done((bf16[2,4,8192]{2,1,0:T(4,128)(2,1)S(1)}, bf16[2,4,8192]{2,1,0:T(4,128)(2,1)S(1)}, u32[]{:S(2)}, u32[]{:S(2)}) %collective-permute-start.4) | collective-permute-done | bytes 131104 | tf_op jit(solution)/shard_map/ppermute | solution.py:36
  20.2 2.2 %collective-permute-done.1.refs_9_ = bf16[2064,128]{1,0:T(8,128)(2,1)S(1)} collective-permute-done((bf16[2064,128]{1,0:T(8,128)(2,1)S(1)}, bf16[2064,128]{1,0:T(8,128)(2,1)S(1)}, u32[]{:S(2)}, u32[]{:S(2)}) %collective-permute-start.1) | collective-permute-done | bytes 528416 | tf_op jit(solution)/shard_map/ppermute | solution.py:36
  22.7 3.1 %collective-permute-start.7 = (bf16[2064,128]{1,0:T(8,128)(2,1)S(1)}, bf16[2064,128]{1,0:T(8,128)(2,1)S(1)}, u32[]{:S(2)}, u32[]{:S(2)}) collective-permute-start(bf16[2064,128]{1,0:T(8,128)(2,1)S(1)} %collective-permute-done.2.refs_6_), channel_id=1, source_target_pairs={{0,196},{1,197},{2,198},{3,199},{8,204},{9,205},{10,206},{11,207},... | collective-permute-start | bytes 1585160 | tf_op jit(solution)/shard_map/ppermute | solution.py:36
  25.8 1.6 %collective-permute-start.10 = (bf16[2,16,8192]{2,1,0:T(8,128)(2,1)S(1)}, bf16[2,16,8192]{2,1,0:T(8,128)(2,1)S(1)}, u32[]{:S(2)}, u32[]{:S(2)}) collective-permute-start(bf16[2,16,8192]{2,1,0:T(8,128)(2,1)S(1)} %pad_maximum_fusion), channel_id=1, source_target_pairs={{0,8},{1,9},{2,10},{3,11},{8,16},{9,17},{10,18},{11,19},{16,24},{1... | collective-permute-start | bytes 1572872 | tf_op jit(solution)/shard_map/ppermute | solution.py:36
  27.4 1.7 %collective-permute-start.8 = (bf16[2,16,8192]{2,1,0:T(8,128)(2,1)S(1)}, bf16[2,16,8192]{2,1,0:T(8,128)(2,1)S(1)}, u32[]{:S(2)}, u32[]{:S(2)}) collective-permute-start(bf16[2,16,8192]{2,1,0:T(8,128)(2,1)S(1)} %pad_maximum_fusion), channel_id=1, source_target_pairs={{0,24},{1,25},{2,26},{3,27},{8,0},{9,1},{10,2},{11,3},{16,8},{17,9... | collective-permute-start | bytes 1572872 | tf_op jit(solution)/shard_map/ppermute | solution.py:36
  29.0 2.0 %collective-permute-start.9 = (bf16[2,16,8192]{2,1,0:T(8,128)(2,1)S(1)}, bf16[2,16,8192]{2,1,0:T(8,128)(2,1)S(1)}, u32[]{:S(2)}, u32[]{:S(2)}) collective-permute-start(bf16[2,16,8192]{2,1,0:T(8,128)(2,1)S(1)} %pad_maximum_fusion), channel_id=1, source_target_pairs={{0,16},{1,17},{2,18},{3,19},{8,24},{9,25},{10,26},{11,27},{16,0},{... | collective-permute-start | bytes 1572872 | tf_op jit(solution)/shard_map/ppermute | solution.py:36
  31.0 5.9 %collective-permute-done.7.refs_7_ = bf16[2064,128]{1,0:T(8,128)(2,1)S(1)} collective-permute-done((bf16[2064,128]{1,0:T(8,128)(2,1)S(1)}, bf16[2064,128]{1,0:T(8,128)(2,1)S(1)}, u32[]{:S(2)}, u32[]{:S(2)}) %collective-permute-start.7) | collective-permute-done | bytes 528416 | tf_op jit(solution)/shard_map/ppermute | solution.py:36
  37.0 3.8 %collective-permute-start.11 = (bf16[2048,128]{1,0:T(8,128)(2,1)S(1)}, bf16[2048,128]{1,0:T(8,128)(2,1)S(1)}, u32[]{:S(2)}, u32[]{:S(2)}) collective-permute-start(bf16[2048,128]{1,0:T(8,128)(2,1)S(1)} %slice.113), channel_id=1, source_target_pairs={{0,196},{1,197},{2,198},{3,199},{8,204},{9,205},{10,206},{11,207},... | collective-permute-start | bytes 1572872 | tf_op jit(solution)/shard_map/ppermute | solution.py:36
  42.2 10.5 %collective-permute-done.9 = bf16[2,16,8192]{2,1,0:T(8,128)(2,1)S(1)} collective-permute-done((bf16[2,16,8192]{2,1,0:T(8,128)(2,1)S(1)}, bf16[2,16,8192]{2,1,0:T(8,128)(2,1)S(1)}, u32[]{:S(2)}, u32[]{:S(2)}) %collective-permute-start.9) | collective-permute-done | bytes 524320 | tf_op jit(solution)/shard_map/ppermute | solution.py:36
  52.7 1.8 %collective-permute-done.12.refs_11_ = bf16[2048,128]{1,0:T(8,128)(2,1)} collective-permute-done((bf16[2048,128]{1,0:T(8,128)(2,1)S(1)}, bf16[2048,128]{1,0:T(8,128)(2,1)}, u32[]{:S(2)}, u32[]{:S(2)}) %collective-permute-start.12) | collective-permute-done | bytes 524320 | tf_op jit(solution)/shard_map/ppermute | solution.py:36
  56.6 1.7 %collective-permute-start.14 = (bf16[1024,128]{1,0:T(8,128)(2,1)S(1)}, bf16[1024,128]{1,0:T(8,128)(2,1)S(1)}, u32[]{:S(2)}, u32[]{:S(2)}) collective-permute-start(bf16[1024,128]{1,0:T(8,128)(2,1)S(1)} %slice.115), channel_id=1, source_target_pairs={{0,196},{1,197},{2,198},{3,199},{8,204},{9,205},{10,206},{11,207},... | collective-permute-start | bytes 786440 | tf_op jit(solution)/shard_map/ppermute | solution.py:36
  60.7 4.6 %collective-permute-done.14.refs_12_ = bf16[1024,128]{1,0:T(8,128)(2,1)S(1)} collective-permute-done((bf16[1024,128]{1,0:T(8,128)(2,1)S(1)}, bf16[1024,128]{1,0:T(8,128)(2,1)S(1)}, u32[]{:S(2)}, u32[]{:S(2)}) %collective-permute-start.14) | collective-permute-done | bytes 262176 | tf_op jit(solution)/shard_map/ppermute | solution.py:36
  65.3 3.8 %collective-permute-done.15.refs_13_ = bf16[1024,128]{1,0:T(8,128)(2,1)S(1)} collective-permute-done((bf16[1024,128]{1,0:T(8,128)(2,1)S(1)}, bf16[1024,128]{1,0:T(8,128)(2,1)S(1)}, u32[]{:S(2)}, u32[]{:S(2)}) %collective-permute-start.15) | collective-permute-done | bytes 262176 | tf_op jit(solution)/shard_map/ppermute | solution.py:36
  69.8 12.5 %shard_map.93 = (bf16[16,128,128]{2,1,0:T(8,128)(2,1)}, bf16[16,128,128]{2,1,0:T(8,128)(2,1)}, bf16[16,128,128]{2,1,0:T(8,128)(2,1)}, bf16[16,128,128]{2,1,0:T(8...) custom-call(s32[1]{0:T(128)} %bitcast.refs_0_, ...), custom_call_target="tpu_custom_call" | custom-call | flops 1700000000 | bytes 16000000 | tf_op jit(solution)/shard_map/pallas_call | solution.py:158
  82.5 2.0 %collective-permute-start.20 = (bf16[8,128,128]{2,1,0:T(8,128)(2,1)}, bf16[8,128,128]{2,1,0:T(8,128)(2,1)S(1)}, u32[]{:S(2)}, u32[]{:S(2)}) collective-permute-start(bf16[8,128,128]{2,1,0:T(8,128)(2,1)} %get-tuple-element.53), channel_id=1, source_target_pairs={{0,64},{1,65},{2,66},{3,67},{8,72},{9,73},{10,74},{11,75},{16,80},... | collective-permute-start | bytes 786440 | tf_op jit(solution)/shard_map/ppermute | solution.py:36
  84.6 6.8 %collective-permute-done.22 = bf16[8,128,128]{2,1,0:T(8,128)(2,1)S(1)} collective-permute-done((bf16[8,128,128]{2,1,0:T(8,128)(2,1)}, bf16[8,128,128]{2,1,0:T(8,128)(2,1)S(1)}, u32[]{:S(2)}, u32[]{:S(2)}) %collective-permute-start.22) | collective-permute-done | bytes 262176 | tf_op jit(solution)/shard_map/ppermute | solution.py:36
  92.5 1.6 %collective-permute-start.23 = (bf16[16,128,128]{2,1,0:T(8,128)(2,1)S(1)}, bf16[16,128,128]{2,1,0:T(8,128)(2,1)S(1)}, u32[]{:S(2)}, u32[]{:S(2)}) collective-permute-start(bf16[16,128,128]{2,1,0:T(8,128)(2,1)S(1)} %add_convert_fusion.5), channel_id=1, source_target_pairs={{0,196},{1,197},{2,198},{3,199},{8,204},{9,205},{10,206},{11,207},... | collective-permute-start | bytes 1572872 | tf_op jit(solution)/shard_map/ppermute | solution.py:36
  97.5 2.1 %collective-permute-start.18 = (bf16[2,16,8192]{2,1,0:T(8,128)(2,1)S(1)}, bf16[2,16,8192]{2,1,0:T(8,128)(2,1)S(1)}, u32[]{:S(2)}, u32[]{:S(2)}) collective-permute-start(bf16[2,16,8192]{2,1,0:T(8,128)(2,1)S(1)} %get-tuple-element.73), channel_id=1, source_target_pairs={{0,24},{1,25},{2,26},{3,27},{8,0},{9,1},{10,2},{11,3},{16,8},{17,9... | collective-permute-start | bytes 1572872 | tf_op jit(solution)/shard_map/ppermute | solution.py:36
  99.7 6.4 %collective-permute-done.23 = bf16[16,128,128]{2,1,0:T(8,128)(2,1)S(1)} collective-permute-done((bf16[16,128,128]{2,1,0:T(8,128)(2,1)S(1)}, bf16[16,128,128]{2,1,0:T(8,128)(2,1)S(1)}, u32[]{:S(2)}, u32[]{:S(2)}) %collective-permute-start.23) | collective-permute-done | bytes 524320 | tf_op jit(solution)/shard_map/ppermute | solution.py:36
  107.0 2.8 %collective-permute-done.21 = bf16[16,128,128]{2,1,0:T(8,128)(2,1)S(1)} collective-permute-done((bf16[16,128,128]{2,1,0:T(8,128)(2,1)S(1)}, bf16[16,128,128]{2,1,0:T(8,128)(2,1)S(1)}, u32[]{:S(2)}, u32[]{:S(2)}) %collective-permute-start.21) | collective-permute-done | bytes 524320 | tf_op jit(solution)/shard_map/ppermute | solution.py:36
  110.8 2.6 %collective-permute-start.25 = (bf16[16,128,128]{2,1,0:T(8,128)(2,1)}, bf16[16,128,128]{2,1,0:T(8,128)(2,1)}, u32[]{:S(2)}, u32[]{:S(2)}) collective-permute-start(bf16[16,128,128]{2,1,0:T(8,128)(2,1)} %add_convert_fusion.4), channel_id=1, source_target_pairs={{0,196},{1,197},{2,198},{3,199},{8,204},{9,205},{10,206},{11,207},... | collective-permute-start | bytes 1572872 | tf_op jit(solution)/shard_map/ppermute | solution.py:36
  113.4 1.8 %collective-permute-start.19 = (bf16[2,16,8192]{2,1,0:T(8,128)(2,1)S(1)}, bf16[2,16,8192]{2,1,0:T(8,128)(2,1)S(1)}, u32[]{:S(2)}, u32[]{:S(2)}) collective-permute-start(bf16[2,16,8192]{2,1,0:T(8,128)(2,1)S(1)} %get-tuple-element.50), channel_id=1, source_target_pairs={{0,16},{1,17},{2,18},{3,19},{8,24},{9,25},{10,26},{11,27},{16,0},{... | collective-permute-start | bytes 1572872 | tf_op jit(solution)/shard_map/ppermute | solution.py:36
  115.3 8.4 %collective-permute-done.25 = bf16[16,128,128]{2,1,0:T(8,128)(2,1)} collective-permute-done((bf16[16,128,128]{2,1,0:T(8,128)(2,1)}, bf16[16,128,128]{2,1,0:T(8,128)(2,1)}, u32[]{:S(2)}, u32[]{:S(2)}) %collective-permute-start.25) | collective-permute-done | bytes 524320 | tf_op jit(solution)/shard_map/ppermute | solution.py:36
  124.8 2.1 %collective-permute-done.24 = bf16[16,128,128]{2,1,0:T(8,128)(2,1)} collective-permute-done((bf16[16,128,128]{2,1,0:T(8,128)(2,1)}, bf16[16,128,128]{2,1,0:T(8,128)(2,1)}, u32[]{:S(2)}, u32[]{:S(2)}) %collective-permute-start.24) | collective-permute-done | bytes 524320 | tf_op jit(solution)/shard_map/ppermute | solution.py:36
  128.2 3.2 %collective-permute-start.30 = (bf16[16,128,128]{2,1,0:T(8,128)(2,1)S(1)}, bf16[16,128,128]{2,1,0:T(8,128)(2,1)S(1)}, u32[]{:S(2)}, u32[]{:S(2)}) collective-permute-start(bf16[16,128,128]{2,1,0:T(8,128)(2,1)S(1)} %add_convert_fusion.1), channel_id=1, source_target_pairs={{0,196},{1,197},{2,198},{3,199},{8,204},{9,205},{10,206},{11,207},... | collective-permute-start | bytes 1572872 | tf_op jit(solution)/shard_map/ppermute | solution.py:36
  131.8 1.5 %collective-permute-start.26 = (bf16[2,4,8192]{2,1,0:T(4,128)(2,1)S(1)}, bf16[2,4,8192]{2,1,0:T(4,128)(2,1)S(1)}, u32[]{:S(2)}, u32[]{:S(2)}) collective-permute-start(bf16[2,4,8192]{2,1,0:T(4,128)(2,1)S(1)} %get-tuple-element.82), channel_id=1, source_target_pairs={{0,1},{1,2},{2,3},{3,0},{8,9},{9,10},{10,11},{11,8},{16,17},{17,18... | collective-permute-start | bytes 393224 | tf_op jit(solution)/shard_map/ppermute | solution.py:36
  134.5 2.2 %collective-permute-start.28 = (bf16[2,4,8192]{2,1,0:T(4,128)(2,1)S(1)}, bf16[2,4,8192]{2,1,0:T(4,128)(2,1)S(1)}, u32[]{:S(2)}, u32[]{:S(2)}) collective-permute-start(bf16[2,4,8192]{2,1,0:T(4,128)(2,1)S(1)} %get-tuple-element.80), channel_id=1, source_target_pairs={{0,3},{1,0},{2,1},{3,2},{8,11},{9,8},{10,9},{11,10},{16,19},{17,16... | collective-permute-start | bytes 393224 | tf_op jit(solution)/shard_map/ppermute | solution.py:36
  136.7 3.7 %collective-permute-done.29 = bf16[16,128,128]{2,1,0:T(8,128)(2,1)S(1)} collective-permute-done((bf16[16,128,128]{2,1,0:T(8,128)(2,1)S(1)}, bf16[16,128,128]{2,1,0:T(8,128)(2,1)S(1)}, u32[]{:S(2)}, u32[]{:S(2)}) %collective-permute-start.29) | collective-permute-done | bytes 524320 | tf_op jit(solution)/shard_map/ppermute | solution.py:36
  (108 shorter events, 25.7 us)
Async XLA Ops:
  1.9 1.7 %collective-permute-start = (bf16[2,2,2,128,128]{4,3,1,0,2:T(8,128)(2,1)S(1)}, bf16[2,2,2,128,128]{4,3,1,0,2:T(8,128)(2,1)S(1)}, u32[]{:S(2)}, u32[]{:S(2)}) collective-permute-start(bf16[2,2,2,128,128]{4,3,1,0,2:T(8,128)(2,1)S(1)} %get-tuple-element.85), channel_id=1, source_target_pairs={{0,32},{1,33},{2,34},{3,35},{8,40},{9,41},{10,42},{11,43},{16,48},... | collective-permute-start | bytes 786440 | tf_op jit(solution)/shard_map/ppermute | solution.py:36
  3.7 18.6 %collective-permute-start.1 = (bf16[2064,128]{1,0:T(8,128)(2,1)S(1)}, bf16[2064,128]{1,0:T(8,128)(2,1)S(1)}, u32[]{:S(2)}, u32[]{:S(2)}) collective-permute-start(bf16[2064,128]{1,0:T(8,128)(2,1)S(1)} %fusion.1.refs_5_), channel_id=1, source_target_pairs={{0,64},{1,65},{2,66},{3,67},{8,72},{9,73},{10,74},{11,75},{16,80},... | collective-permute-start | bytes 1585160 | tf_op jit(solution)/shard_map/ppermute | solution.py:36
  5.7 16.6 %collective-permute-start.2 = (bf16[2064,128]{1,0:T(8,128)(2,1)S(1)}, bf16[2064,128]{1,0:T(8,128)(2,1)S(1)}, u32[]{:S(2)}, u32[]{:S(2)}) collective-permute-start(bf16[2064,128]{1,0:T(8,128)(2,1)S(1)} %fusion.1.refs_5_), channel_id=1, source_target_pairs={{0,196},{1,197},{2,198},{3,199},{8,204},{9,205},{10,206},{11,207},... | collective-permute-start | bytes 1585160 | tf_op jit(solution)/shard_map/ppermute | solution.py:36
  9.9 5.7 %collective-permute-start.3 = (bf16[2,4,8192]{2,1,0:T(4,128)(2,1)S(1)}, bf16[2,4,8192]{2,1,0:T(4,128)(2,1)S(1)}, u32[]{:S(2)}, u32[]{:S(2)}) collective-permute-start(bf16[2,4,8192]{2,1,0:T(4,128)(2,1)S(1)} %pad_maximum_fusion.1), channel_id=1, source_target_pairs={{0,3},{1,0},{2,1},{3,2},{8,11},{9,8},{10,9},{11,10},{16,19},{17,16... | collective-permute-start | bytes 393224 | tf_op jit(solution)/shard_map/ppermute | solution.py:36
  10.5 8.8 %collective-permute-start.4 = (bf16[2,4,8192]{2,1,0:T(4,128)(2,1)S(1)}, bf16[2,4,8192]{2,1,0:T(4,128)(2,1)S(1)}, u32[]{:S(2)}, u32[]{:S(2)}) collective-permute-start(bf16[2,4,8192]{2,1,0:T(4,128)(2,1)S(1)} %pad_maximum_fusion.1), channel_id=1, source_target_pairs={{0,2},{1,3},{2,0},{3,1},{8,10},{9,11},{10,8},{11,9},{16,18},{17,19... | collective-permute-start | bytes 393224 | tf_op jit(solution)/shard_map/ppermute | solution.py:36
  12.9 7.3 %collective-permute-start.5 = (bf16[2,4,8192]{2,1,0:T(4,128)(2,1)S(1)}, bf16[2,4,8192]{2,1,0:T(4,128)(2,1)S(1)}, u32[]{:S(2)}, u32[]{:S(2)}) collective-permute-start(bf16[2,4,8192]{2,1,0:T(4,128)(2,1)S(1)} %pad_maximum_fusion.1), channel_id=1, source_target_pairs={{0,1},{1,2},{2,3},{3,0},{8,9},{9,10},{10,11},{11,8},{16,17},{17,18... | collective-permute-start | bytes 393224 | tf_op jit(solution)/shard_map/ppermute | solution.py:36
  22.7 14.3 %collective-permute-start.7 = (bf16[2064,128]{1,0:T(8,128)(2,1)S(1)}, bf16[2064,128]{1,0:T(8,128)(2,1)S(1)}, u32[]{:S(2)}, u32[]{:S(2)}) collective-permute-start(bf16[2064,128]{1,0:T(8,128)(2,1)S(1)} %collective-permute-done.2.refs_6_), channel_id=1, source_target_pairs={{0,196},{1,197},{2,198},{3,199},{8,204},{9,205},{10,206},{11,207},... | collective-permute-start | bytes 1585160 | tf_op jit(solution)/shard_map/ppermute | solution.py:36
  25.8 15.0 %collective-permute-start.6 = (bf16[2064,128]{1,0:T(8,128)(2,1)S(1)}, bf16[2064,128]{1,0:T(8,128)(2,1)S(1)}, u32[]{:S(2)}, u32[]{:S(2)}) collective-permute-start(bf16[2064,128]{1,0:T(8,128)(2,1)S(1)} %collective-permute-done.1.refs_9_), channel_id=1, source_target_pairs={{0,64},{1,65},{2,66},{3,67},{8,72},{9,73},{10,74},{11,75},{16,80},... | collective-permute-start | bytes 1585160 | tf_op jit(solution)/shard_map/ppermute | solution.py:36
  25.8 15.1 %collective-permute-start.10 = (bf16[2,16,8192]{2,1,0:T(8,128)(2,1)S(1)}, bf16[2,16,8192]{2,1,0:T(8,128)(2,1)S(1)}, u32[]{:S(2)}, u32[]{:S(2)}) collective-permute-start(bf16[2,16,8192]{2,1,0:T(8,128)(2,1)S(1)} %pad_maximum_fusion), channel_id=1, source_target_pairs={{0,8},{1,9},{2,10},{3,11},{8,16},{9,17},{10,18},{11,19},{16,24},{1... | collective-permute-start | bytes 1572872 | tf_op jit(solution)/shard_map/ppermute | solution.py:36
  27.4 14.9 %collective-permute-start.8 = (bf16[2,16,8192]{2,1,0:T(8,128)(2,1)S(1)}, bf16[2,16,8192]{2,1,0:T(8,128)(2,1)S(1)}, u32[]{:S(2)}, u32[]{:S(2)}) collective-permute-start(bf16[2,16,8192]{2,1,0:T(8,128)(2,1)S(1)} %pad_maximum_fusion), channel_id=1, source_target_pairs={{0,24},{1,25},{2,26},{3,27},{8,0},{9,1},{10,2},{11,3},{16,8},{17,9... | collective-permute-start | bytes 1572872 | tf_op jit(solution)/shard_map/ppermute | solution.py:36
  29.0 23.7 %collective-permute-start.9 = (bf16[2,16,8192]{2,1,0:T(8,128)(2,1)S(1)}, bf16[2,16,8192]{2,1,0:T(8,128)(2,1)S(1)}, u32[]{:S(2)}, u32[]{:S(2)}) collective-permute-start(bf16[2,16,8192]{2,1,0:T(8,128)(2,1)S(1)} %pad_maximum_fusion), channel_id=1, source_target_pairs={{0,16},{1,17},{2,18},{3,19},{8,24},{9,25},{10,26},{11,27},{16,0},{... | collective-permute-start | bytes 1572872 | tf_op jit(solution)/shard_map/ppermute | solution.py:36
  37.0 15.8 %collective-permute-start.11 = (bf16[2048,128]{1,0:T(8,128)(2,1)S(1)}, bf16[2048,128]{1,0:T(8,128)(2,1)S(1)}, u32[]{:S(2)}, u32[]{:S(2)}) collective-permute-start(bf16[2048,128]{1,0:T(8,128)(2,1)S(1)} %slice.113), channel_id=1, source_target_pairs={{0,196},{1,197},{2,198},{3,199},{8,204},{9,205},{10,206},{11,207},... | collective-permute-start | bytes 1572872 | tf_op jit(solution)/shard_map/ppermute | solution.py:36
  40.8 13.8 %collective-permute-start.12 = (bf16[2048,128]{1,0:T(8,128)(2,1)S(1)}, bf16[2048,128]{1,0:T(8,128)(2,1)}, u32[]{:S(2)}, u32[]{:S(2)}) collective-permute-start(bf16[2048,128]{1,0:T(8,128)(2,1)S(1)} %slice.114), channel_id=1, source_target_pairs={{0,64},{1,65},{2,66},{3,67},{8,72},{9,73},{10,74},{11,75},{16,80},... | collective-permute-start | bytes 1572872 | tf_op jit(solution)/shard_map/ppermute | solution.py:36
  54.7 14.4 %collective-permute-start.13 = (bf16[2,64,8192]{2,1,0:T(8,128)(2,1)S(1)}, bf16[2,64,8192]{2,1,0:T(8,128)(2,1)}, u32[]{:S(2)}, u32[]{:S(2)}) collective-permute-start(bf16[2,64,8192]{2,1,0:T(8,128)(2,1)S(1)} %constant_dynamic-update-slice_fusion.refs_3_), channel_id=1, source_target_pairs={{0,32},{1,33},{2,34},{3,35},{8,40},{9,41},{10,42},{11,43},{16,48},... | collective-permute-start | bytes 6291464 | tf_op jit(solution)/shard_map/ppermute | solution.py:36
  56.6 8.7 %collective-permute-start.14 = (bf16[1024,128]{1,0:T(8,128)(2,1)S(1)}, bf16[1024,128]{1,0:T(8,128)(2,1)S(1)}, u32[]{:S(2)}, u32[]{:S(2)}) collective-permute-start(bf16[1024,128]{1,0:T(8,128)(2,1)S(1)} %slice.115), channel_id=1, source_target_pairs={{0,196},{1,197},{2,198},{3,199},{8,204},{9,205},{10,206},{11,207},... | collective-permute-start | bytes 786440 | tf_op jit(solution)/shard_map/ppermute | solution.py:36
  59.2 9.9 %collective-permute-start.15 = (bf16[1024,128]{1,0:T(8,128)(2,1)S(1)}, bf16[1024,128]{1,0:T(8,128)(2,1)S(1)}, u32[]{:S(2)}, u32[]{:S(2)}) collective-permute-start(bf16[1024,128]{1,0:T(8,128)(2,1)S(1)} %slice.116), channel_id=1, source_target_pairs={{0,64},{1,65},{2,66},{3,67},{8,72},{9,73},{10,74},{11,75},{16,80},... | collective-permute-start | bytes 786440 | tf_op jit(solution)/shard_map/ppermute | solution.py:36
  82.4 13.5 %collective-permute-start.16 = (bf16[2,64,8192]{2,1,0:T(8,128)(2,1)}, bf16[2,64,8192]{2,1,0:T(8,128)(2,1)S(1)}, u32[]{:S(2)}, u32[]{:S(2)}) collective-permute-start(bf16[2,64,8192]{2,1,0:T(8,128)(2,1)} %get-tuple-element.49), channel_id=1, source_target_pairs={{0,32},{1,33},{2,34},{3,35},{8,40},{9,41},{10,42},{11,43},{16,48},... | collective-permute-start | bytes 6291464 | tf_op jit(solution)/shard_map/ppermute | solution.py:36
  82.5 8.9 %collective-permute-start.22 = (bf16[8,128,128]{2,1,0:T(8,128)(2,1)}, bf16[8,128,128]{2,1,0:T(8,128)(2,1)S(1)}, u32[]{:S(2)}, u32[]{:S(2)}) collective-permute-start(bf16[8,128,128]{2,1,0:T(8,128)(2,1)} %get-tuple-element.56), channel_id=1, source_target_pairs={{0,196},{1,197},{2,198},{3,199},{8,204},{9,205},{10,206},{11,207},... | collective-permute-start | bytes 786440 | tf_op jit(solution)/shard_map/ppermute | solution.py:36
  82.5 11.5 %collective-permute-start.20 = (bf16[8,128,128]{2,1,0:T(8,128)(2,1)}, bf16[8,128,128]{2,1,0:T(8,128)(2,1)S(1)}, u32[]{:S(2)}, u32[]{:S(2)}) collective-permute-start(bf16[8,128,128]{2,1,0:T(8,128)(2,1)} %get-tuple-element.53), channel_id=1, source_target_pairs={{0,64},{1,65},{2,66},{3,67},{8,72},{9,73},{10,74},{11,75},{16,80},... | collective-permute-start | bytes 786440 | tf_op jit(solution)/shard_map/ppermute | solution.py:36
  92.5 13.6 %collective-permute-start.23 = (bf16[16,128,128]{2,1,0:T(8,128)(2,1)S(1)}, bf16[16,128,128]{2,1,0:T(8,128)(2,1)S(1)}, u32[]{:S(2)}, u32[]{:S(2)}) collective-permute-start(bf16[16,128,128]{2,1,0:T(8,128)(2,1)S(1)} %add_convert_fusion.5), channel_id=1, source_target_pairs={{0,196},{1,197},{2,198},{3,199},{8,204},{9,205},{10,206},{11,207},... | collective-permute-start | bytes 1572872 | tf_op jit(solution)/shard_map/ppermute | solution.py:36
  95.2 14.7 %collective-permute-start.21 = (bf16[16,128,128]{2,1,0:T(8,128)(2,1)S(1)}, bf16[16,128,128]{2,1,0:T(8,128)(2,1)S(1)}, u32[]{:S(2)}, u32[]{:S(2)}) collective-permute-start(bf16[16,128,128]{2,1,0:T(8,128)(2,1)S(1)} %add_convert_fusion.7), channel_id=1, source_target_pairs={{0,64},{1,65},{2,66},{3,67},{8,72},{9,73},{10,74},{11,75},{16,80},... | collective-permute-start | bytes 1572872 | tf_op jit(solution)/shard_map/ppermute | solution.py:36
  96.3 14.5 %collective-permute-start.17 = (bf16[2,16,8192]{2,1,0:T(8,128)(2,1)S(1)}, bf16[2,16,8192]{2,1,0:T(8,128)(2,1)S(1)}, u32[]{:S(2)}, u32[]{:S(2)}) collective-permute-start(bf16[2,16,8192]{2,1,0:T(8,128)(2,1)S(1)} %get-tuple-element.74), channel_id=1, source_target_pairs={{0,8},{1,9},{2,10},{3,11},{8,16},{9,17},{10,18},{11,19},{16,24},{1... | collective-permute-start | bytes 1572872 | tf_op jit(solution)/shard_map/ppermute | solution.py:36
  97.5 13.3 %collective-permute-start.18 = (bf16[2,16,8192]{2,1,0:T(8,128)(2,1)S(1)}, bf16[2,16,8192]{2,1,0:T(8,128)(2,1)S(1)}, u32[]{:S(2)}, u32[]{:S(2)}) collective-permute-start(bf16[2,16,8192]{2,1,0:T(8,128)(2,1)S(1)} %get-tuple-element.73), channel_id=1, source_target_pairs={{0,24},{1,25},{2,26},{3,27},{8,0},{9,1},{10,2},{11,3},{16,8},{17,9... | collective-permute-start | bytes 1572872 | tf_op jit(solution)/shard_map/ppermute | solution.py:36
  110.8 12.8 %collective-permute-start.25 = (bf16[16,128,128]{2,1,0:T(8,128)(2,1)}, bf16[16,128,128]{2,1,0:T(8,128)(2,1)}, u32[]{:S(2)}, u32[]{:S(2)}) collective-permute-start(bf16[16,128,128]{2,1,0:T(8,128)(2,1)} %add_convert_fusion.4), channel_id=1, source_target_pairs={{0,196},{1,197},{2,198},{3,199},{8,204},{9,205},{10,206},{11,207},... | collective-permute-start | bytes 1572872 | tf_op jit(solution)/shard_map/ppermute | solution.py:36
  113.4 13.4 %collective-permute-start.24 = (bf16[16,128,128]{2,1,0:T(8,128)(2,1)}, bf16[16,128,128]{2,1,0:T(8,128)(2,1)}, u32[]{:S(2)}, u32[]{:S(2)}) collective-permute-start(bf16[16,128,128]{2,1,0:T(8,128)(2,1)} %add_convert_fusion.6), channel_id=1, source_target_pairs={{0,64},{1,65},{2,66},{3,67},{8,72},{9,73},{10,74},{11,75},{16,80},... | collective-permute-start | bytes 1572872 | tf_op jit(solution)/shard_map/ppermute | solution.py:36
  113.4 14.6 %collective-permute-start.19 = (bf16[2,16,8192]{2,1,0:T(8,128)(2,1)S(1)}, bf16[2,16,8192]{2,1,0:T(8,128)(2,1)S(1)}, u32[]{:S(2)}, u32[]{:S(2)}) collective-permute-start(bf16[2,16,8192]{2,1,0:T(8,128)(2,1)S(1)} %get-tuple-element.50), channel_id=1, source_target_pairs={{0,16},{1,17},{2,18},{3,19},{8,24},{9,25},{10,26},{11,27},{16,0},{... | collective-permute-start | bytes 1572872 | tf_op jit(solution)/shard_map/ppermute | solution.py:36
  128.1 12.3 %collective-permute-start.29 = (bf16[16,128,128]{2,1,0:T(8,128)(2,1)S(1)}, bf16[16,128,128]{2,1,0:T(8,128)(2,1)S(1)}, u32[]{:S(2)}, u32[]{:S(2)}) collective-permute-start(bf16[16,128,128]{2,1,0:T(8,128)(2,1)S(1)} %add_convert_fusion.2), channel_id=1, source_target_pairs={{0,64},{1,65},{2,66},{3,67},{8,72},{9,73},{10,74},{11,75},{16,80},... | collective-permute-start | bytes 1572872 | tf_op jit(solution)/shard_map/ppermute | solution.py:36
  128.2 12.2 %collective-permute-start.30 = (bf16[16,128,128]{2,1,0:T(8,128)(2,1)S(1)}, bf16[16,128,128]{2,1,0:T(8,128)(2,1)S(1)}, u32[]{:S(2)}, u32[]{:S(2)}) collective-permute-start(bf16[16,128,128]{2,1,0:T(8,128)(2,1)S(1)} %add_convert_fusion.1), channel_id=1, source_target_pairs={{0,196},{1,197},{2,198},{3,199},{8,204},{9,205},{10,206},{11,207},... | collective-permute-start | bytes 1572872 | tf_op jit(solution)/shard_map/ppermute | solution.py:36
  131.8 8.9 %collective-permute-start.26 = (bf16[2,4,8192]{2,1,0:T(4,128)(2,1)S(1)}, bf16[2,4,8192]{2,1,0:T(4,128)(2,1)S(1)}, u32[]{:S(2)}, u32[]{:S(2)}) collective-permute-start(bf16[2,4,8192]{2,1,0:T(4,128)(2,1)S(1)} %get-tuple-element.82), channel_id=1, source_target_pairs={{0,1},{1,2},{2,3},{3,0},{8,9},{9,10},{10,11},{11,8},{16,17},{17,18... | collective-permute-start | bytes 393224 | tf_op jit(solution)/shard_map/ppermute | solution.py:36
  133.4 7.4 %collective-permute-start.27 = (bf16[2,4,8192]{2,1,0:T(4,128)(2,1)S(1)}, bf16[2,4,8192]{2,1,0:T(4,128)(2,1)S(1)}, u32[]{:S(2)}, u32[]{:S(2)}) collective-permute-start(bf16[2,4,8192]{2,1,0:T(4,128)(2,1)S(1)} %get-tuple-element.81), channel_id=1, source_target_pairs={{0,2},{1,3},{2,0},{3,1},{8,10},{9,11},{10,8},{11,9},{16,18},{17,19... | collective-permute-start | bytes 393224 | tf_op jit(solution)/shard_map/ppermute | solution.py:36
  134.5 6.4 %collective-permute-start.28 = (bf16[2,4,8192]{2,1,0:T(4,128)(2,1)S(1)}, bf16[2,4,8192]{2,1,0:T(4,128)(2,1)S(1)}, u32[]{:S(2)}, u32[]{:S(2)}) collective-permute-start(bf16[2,4,8192]{2,1,0:T(4,128)(2,1)S(1)} %get-tuple-element.80), channel_id=1, source_target_pairs={{0,3},{1,0},{2,1},{3,2},{8,11},{9,8},{10,9},{11,10},{16,19},{17,16... | collective-permute-start | bytes 393224 | tf_op jit(solution)/shard_map/ppermute | solution.py:36
  140.7 1.6 %collective-permute-start.31 = (bf16[2,2,2,128,128]{4,3,1,0,2:T(8,128)(2,1)S(1)}, bf16[2,2,2,128,128]{4,3,1,0,2:T(8,128)(2,1)S(1)}, u32[]{:S(2)}, u32[]{:S(2)}) collective-permute-start(bf16[2,2,2,128,128]{4,3,1,0,2:T(8,128)(2,1)S(1)} %bitcast.34), channel_id=1, source_target_pairs={{0,32},{1,33},{2,34},{3,35},{8,40},{9,41},{10,42},{11,43},{16,48},... | collective-permute-start | bytes 786440 | tf_op jit(solution)/shard_map/ppermute | solution.py:36
  (18 other events, 276.2 us)

commit v2 on v1

--- a/solution.py
+++ b/solution.py
@@ -220,16 +220,17 @@
     up, down = after(ring_1, rows)
     ring_2 = send(up, dz=-1), send(down, dz=1)
     size = shard.shape[0] - LIST_ROWS
-    ring_3 = send(ring_2[0][:size], dz=-1), send(ring_2[1][:size], dz=1)
+    below, above = [v[1][-LIST_ROWS] for v in (ring_1, ring_2)], [v[0][-LIST_ROWS] for v in (ring_2, ring_1)]
+    far_lists = jnp.where(low < 2, jnp.where(low == 0, *below), jnp.where(low == 2, *above))
+    far_lists = far_lists[: lists.size]
+    up, down = after(ring_2, far_lists)
+    ring_3 = send(up[:size], dz=-1), send(down[:size], dz=1)
     ring_4 = send(ring_3[0][: size // 2], dz=-1), send(ring_3[1][size // 2 :], dz=1)
     weights = [shard, ring_1[0], ring_2[0], ring_3[0], ring_1[1], ring_2[1], ring_3[1], *ring_4]
     rows = after([rows] + [send(rows, dy=-d) for d in (1, 2, 3)], *ring_3)
     rows = jnp.concatenate(rows, axis=1)
     row_pair = [rows, swap_cores(rows)]
 
-    below, above = [v[1][-LIST_ROWS] for v in (ring_1, ring_2)], [v[0][-LIST_ROWS] for v in (ring_2, ring_1)]
-    far_lists = jnp.where(low < 2, jnp.where(low == 0, *below), jnp.where(low == 2, *above))
-    far_lists = far_lists[: lists.size]
     far_lists = far_lists.astype(jnp.int32).reshape(lists.shape)
     lists = lax.dynamic_slice_in_dim(jnp.stack([lists, far_lists]), 2 * core, 2, axis=1).reshape(4, -1)
     index, count = lists[:, :-1], lists[:, -1]

time: 145 us -> 144 us (level)
  waiting for transfers between devices: 66.5 us -> 64.8 us
    ppermute x32, waiting for transfers between devices: 66.5 us -> 64.8 us  [send(): return lax.ppermute(value, ('row', 'col'), pairs)]
  transfers between devices with their start and end apart: 32 -> 32, of which waited for: 17 -> 18; matrix products, arithmetic and copies ran while one was open for 10% -> 10% of each run, Pallas kernels for 0% -> 0%
where the time goes in v2:
time: 144 us; the launch traced here: 142 us
  waiting for transfers between devices  64.8 us (45%)
  starting transfers between devices  46.6 us (32%)
  Pallas kernels  12.5 us (9%)
  other arithmetic  10.9 us (8%)
  local copies, waits for them, and re-layouts  6.33 us (4%)
    ppermute x32, waiting for transfers between devices, send(): return lax.ppermute(value, ('row', 'col'), pairs)  64.8 us
    ppermute x32, starting transfers between devices, send(): return lax.ppermute(value, ('row', 'col'), pairs)  46.6 us
    pallas_call x1, Pallas kernels, products(): pl.pallas_call(functools.partial(products_kernel, slots), out_shape=[jax....  12.5 us
  transfers between devices with their start and end apart: 32, of which 18 were waited for; matrix products, arithmetic and copies ran while one was open for 10% of the time, Pallas kernels for 0%

profile of v2, /device:TPU:2, one launch (start us, length us, event | category | flops | bytes accessed | tf_op | source)
XLA Modules:
  0.0 142.2 jit_solution(15273415894072282928)
XLA Ops:
  3.7 2.0 %collective-permute-start.1 = (bf16[2064,128]{1,0:T(8,128)(2,1)S(1)}, bf16[2064,128]{1,0:T(8,128)(2,1)S(1)}, u32[]{:S(2)}, u32[]{:S(2)}) collective-permute-start(bf16[2064,128]{1,0:T(8,128)(2,1)S(1)} %fusion.1.refs_5_), channel_id=1, source_target_pairs={{0,64},{1,65},{2,66},{3,67},{8,72},{9,73},{10,74},{11,75},{16,80},... | collective-permute-start | bytes 1585160 | tf_op jit(solution)/shard_map/ppermute | solution.py:36
  5.7 4.0 %collective-permute-start.2 = (bf16[2064,128]{1,0:T(8,128)(2,1)S(1)}, bf16[2064,128]{1,0:T(8,128)(2,1)S(1)}, u32[]{:S(2)}, u32[]{:S(2)}) collective-permute-start(bf16[2064,128]{1,0:T(8,128)(2,1)S(1)} %fusion.1.refs_5_), channel_id=1, source_target_pairs={{0,196},{1,197},{2,198},{3,199},{8,204},{9,205},{10,206},{11,207},... | collective-permute-start | bytes 1585160 | tf_op jit(solution)/shard_map/ppermute | solution.py:36
  10.5 2.4 %collective-permute-start.4 = (bf16[2,4,8192]{2,1,0:T(4,128)(2,1)S(1)}, bf16[2,4,8192]{2,1,0:T(4,128)(2,1)S(1)}, u32[]{:S(2)}, u32[]{:S(2)}) collective-permute-start(bf16[2,4,8192]{2,1,0:T(4,128)(2,1)S(1)} %pad_maximum_fusion.1), channel_id=1, source_target_pairs={{0,2},{1,3},{2,0},{3,1},{8,10},{9,11},{10,8},{11,9},{16,18},{17,19... | collective-permute-start | bytes 393224 | tf_op jit(solution)/shard_map/ppermute | solution.py:36
  12.9 1.8 %collective-permute-start.5 = (bf16[2,4,8192]{2,1,0:T(4,128)(2,1)S(1)}, bf16[2,4,8192]{2,1,0:T(4,128)(2,1)S(1)}, u32[]{:S(2)}, u32[]{:S(2)}) collective-permute-start(bf16[2,4,8192]{2,1,0:T(4,128)(2,1)S(1)} %pad_maximum_fusion.1), channel_id=1, source_target_pairs={{0,1},{1,2},{2,3},{3,0},{8,9},{9,10},{10,11},{11,8},{16,17},{17,18... | collective-permute-start | bytes 393224 | tf_op jit(solution)/shard_map/ppermute | solution.py:36
  15.6 3.7 %collective-permute-done.4 = bf16[2,4,8192]{2,1,0:T(4,128)(2,1)S(1)} collective-permute-done((bf16[2,4,8192]{2,1,0:T(4,128)(2,1)S(1)}, bf16[2,4,8192]{2,1,0:T(4,128)(2,1)S(1)}, u32[]{:S(2)}, u32[]{:S(2)}) %collective-permute-start.4) | collective-permute-done | bytes 131104 | tf_op jit(solution)/shard_map/ppermute | solution.py:36
  20.2 2.2 %collective-permute-done.1.refs_9_ = bf16[2064,128]{1,0:T(8,128)(2,1)S(1)} collective-permute-done((bf16[2064,128]{1,0:T(8,128)(2,1)S(1)}, bf16[2064,128]{1,0:T(8,128)(2,1)S(1)}, u32[]{:S(2)}, u32[]{:S(2)}) %collective-permute-start.1) | collective-permute-done | bytes 528416 | tf_op jit(solution)/shard_map/ppermute | solution.py:36
  22.8 3.2 %collective-permute-start.7 = (bf16[2064,128]{1,0:T(8,128)(2,1)S(1)}, bf16[2064,128]{1,0:T(8,128)(2,1)S(1)}, u32[]{:S(2)}, u32[]{:S(2)}) collective-permute-start(bf16[2064,128]{1,0:T(8,128)(2,1)S(1)} %collective-permute-done.2.refs_6_), channel_id=1, source_target_pairs={{0,196},{1,197},{2,198},{3,199},{8,204},{9,205},{10,206},{11,207},... | collective-permute-start | bytes 1585160 | tf_op jit(solution)/shard_map/ppermute | solution.py:36
  26.0 1.6 %collective-permute-start.10 = (bf16[2,16,8192]{2,1,0:T(8,128)(2,1)S(1)}, bf16[2,16,8192]{2,1,0:T(8,128)(2,1)S(1)}, u32[]{:S(2)}, u32[]{:S(2)}) collective-permute-start(bf16[2,16,8192]{2,1,0:T(8,128)(2,1)S(1)} %pad_maximum_fusion), channel_id=1, source_target_pairs={{0,8},{1,9},{2,10},{3,11},{8,16},{9,17},{10,18},{11,19},{16,24},{1... | collective-permute-start | bytes 1572872 | tf_op jit(solution)/shard_map/ppermute | solution.py:36
  27.6 1.7 %collective-permute-start.8 = (bf16[2,16,8192]{2,1,0:T(8,128)(2,1)S(1)}, bf16[2,16,8192]{2,1,0:T(8,128)(2,1)S(1)}, u32[]{:S(2)}, u32[]{:S(2)}) collective-permute-start(bf16[2,16,8192]{2,1,0:T(8,128)(2,1)S(1)} %pad_maximum_fusion), channel_id=1, source_target_pairs={{0,24},{1,25},{2,26},{3,27},{8,0},{9,1},{10,2},{11,3},{16,8},{17,9... | collective-permute-start | bytes 1572872 | tf_op jit(solution)/shard_map/ppermute | solution.py:36
  29.2 2.0 %collective-permute-start.9 = (bf16[2,16,8192]{2,1,0:T(8,128)(2,1)S(1)}, bf16[2,16,8192]{2,1,0:T(8,128)(2,1)S(1)}, u32[]{:S(2)}, u32[]{:S(2)}) collective-permute-start(bf16[2,16,8192]{2,1,0:T(8,128)(2,1)S(1)} %pad_maximum_fusion), channel_id=1, source_target_pairs={{0,16},{1,17},{2,18},{3,19},{8,24},{9,25},{10,26},{11,27},{16,0},{... | collective-permute-start | bytes 1572872 | tf_op jit(solution)/shard_map/ppermute | solution.py:36
  31.2 6.6 %collective-permute-done.6.refs_10_ = bf16[2064,128]{1,0:T(8,128)(2,1)S(1)} collective-permute-done((bf16[2064,128]{1,0:T(8,128)(2,1)S(1)}, bf16[2064,128]{1,0:T(8,128)(2,1)S(1)}, u32[]{:S(2)}, u32[]{:S(2)}) %collective-permute-start.6) | collective-permute-done | bytes 528416 | tf_op jit(solution)/shard_map/ppermute | solution.py:36
  37.8 3.0 %collective-permute-start.11 = (bf16[2048,128]{1,0:T(8,128)(2,1)S(1)}, bf16[2048,128]{1,0:T(8,128)(2,1)S(1)}, u32[]{:S(2)}, u32[]{:S(2)}) collective-permute-start(bf16[2048,128]{1,0:T(8,128)(2,1)S(1)} %slice.89), channel_id=1, source_target_pairs={{0,196},{1,197},{2,198},{3,199},{8,204},{9,205},{10,206},{11,207},... | collective-permute-start | bytes 1572872 | tf_op jit(solution)/shard_map/ppermute | solution.py:36
  42.4 10.4 %collective-permute-done.9 = bf16[2,16,8192]{2,1,0:T(8,128)(2,1)S(1)} collective-permute-done((bf16[2,16,8192]{2,1,0:T(8,128)(2,1)S(1)}, bf16[2,16,8192]{2,1,0:T(8,128)(2,1)S(1)}, u32[]{:S(2)}, u32[]{:S(2)}) %collective-permute-start.9) | collective-permute-done | bytes 524320 | tf_op jit(solution)/shard_map/ppermute | solution.py:36
  52.8 1.7 %collective-permute-done.12.refs_11_ = bf16[2048,128]{1,0:T(8,128)(2,1)} collective-permute-done((bf16[2048,128]{1,0:T(8,128)(2,1)S(1)}, bf16[2048,128]{1,0:T(8,128)(2,1)}, u32[]{:S(2)}, u32[]{:S(2)}) %collective-permute-start.12) | collective-permute-done | bytes 524320 | tf_op jit(solution)/shard_map/ppermute | solution.py:36
  58.2 1.8 %collective-permute-start.15 = (bf16[1024,128]{1,0:T(8,128)(2,1)S(1)}, bf16[1024,128]{1,0:T(8,128)(2,1)S(1)}, u32[]{:S(2)}, u32[]{:S(2)}) collective-permute-start(bf16[1024,128]{1,0:T(8,128)(2,1)S(1)} %slice.114), channel_id=1, source_target_pairs={{0,64},{1,65},{2,66},{3,67},{8,72},{9,73},{10,74},{11,75},{16,80},... | collective-permute-start | bytes 786440 | tf_op jit(solution)/shard_map/ppermute | solution.py:36
  60.8 4.6 %collective-permute-done.14.refs_12_ = bf16[1024,128]{1,0:T(8,128)(2,1)S(1)} collective-permute-done((bf16[1024,128]{1,0:T(8,128)(2,1)S(1)}, bf16[1024,128]{1,0:T(8,128)(2,1)S(1)}, u32[]{:S(2)}, u32[]{:S(2)}) %collective-permute-start.14) | collective-permute-done | bytes 262176 | tf_op jit(solution)/shard_map/ppermute | solution.py:36
  65.3 2.7 %collective-permute-done.15.refs_13_ = bf16[1024,128]{1,0:T(8,128)(2,1)S(1)} collective-permute-done((bf16[1024,128]{1,0:T(8,128)(2,1)S(1)}, bf16[1024,128]{1,0:T(8,128)(2,1)S(1)}, u32[]{:S(2)}, u32[]{:S(2)}) %collective-permute-start.15) | collective-permute-done | bytes 262176 | tf_op jit(solution)/shard_map/ppermute | solution.py:36
  68.8 12.5 %shard_map.93 = (bf16[16,128,128]{2,1,0:T(8,128)(2,1)}, bf16[16,128,128]{2,1,0:T(8,128)(2,1)}, bf16[16,128,128]{2,1,0:T(8,128)(2,1)}, bf16[16,128,128]{2,1,0:T(8...) custom-call(s32[1]{0:T(128)} %bitcast.refs_0_, ...), custom_call_target="tpu_custom_call" | custom-call | flops 1700000000 | bytes 16000000 | tf_op jit(solution)/shard_map/pallas_call | solution.py:158
  81.5 2.0 %collective-permute-start.20 = (bf16[8,128,128]{2,1,0:T(8,128)(2,1)}, bf16[8,128,128]{2,1,0:T(8,128)(2,1)S(1)}, u32[]{:S(2)}, u32[]{:S(2)}) collective-permute-start(bf16[8,128,128]{2,1,0:T(8,128)(2,1)} %get-tuple-element.57), channel_id=1, source_target_pairs={{0,64},{1,65},{2,66},{3,67},{8,72},{9,73},{10,74},{11,75},{16,80},... | collective-permute-start | bytes 786440 | tf_op jit(solution)/shard_map/ppermute | solution.py:36
  83.5 6.8 %collective-permute-done.22 = bf16[8,128,128]{2,1,0:T(8,128)(2,1)S(1)} collective-permute-done((bf16[8,128,128]{2,1,0:T(8,128)(2,1)}, bf16[8,128,128]{2,1,0:T(8,128)(2,1)S(1)}, u32[]{:S(2)}, u32[]{:S(2)}) %collective-permute-start.22) | collective-permute-done | bytes 262176 | tf_op jit(solution)/shard_map/ppermute | solution.py:36
  95.3 1.7 %collective-permute-start.17 = (bf16[2,16,8192]{2,1,0:T(8,128)(2,1)S(1)}, bf16[2,16,8192]{2,1,0:T(8,128)(2,1)S(1)}, u32[]{:S(2)}, u32[]{:S(2)}) collective-permute-start(bf16[2,16,8192]{2,1,0:T(8,128)(2,1)S(1)} %get-tuple-element.78), channel_id=1, source_target_pairs={{0,8},{1,9},{2,10},{3,11},{8,16},{9,17},{10,18},{11,19},{16,24},{1... | collective-permute-start | bytes 1572872 | tf_op jit(solution)/shard_map/ppermute | solution.py:36
  96.9 1.7 %collective-permute-start.18 = (bf16[2,16,8192]{2,1,0:T(8,128)(2,1)S(1)}, bf16[2,16,8192]{2,1,0:T(8,128)(2,1)S(1)}, u32[]{:S(2)}, u32[]{:S(2)}) collective-permute-start(bf16[2,16,8192]{2,1,0:T(8,128)(2,1)S(1)} %get-tuple-element.77), channel_id=1, source_target_pairs={{0,24},{1,25},{2,26},{3,27},{8,0},{9,1},{10,2},{11,3},{16,8},{17,9... | collective-permute-start | bytes 1572872 | tf_op jit(solution)/shard_map/ppermute | solution.py:36
  98.7 6.3 %collective-permute-done.23 = bf16[16,128,128]{2,1,0:T(8,128)(2,1)S(1)} collective-permute-done((bf16[16,128,128]{2,1,0:T(8,128)(2,1)S(1)}, bf16[16,128,128]{2,1,0:T(8,128)(2,1)S(1)}, u32[]{:S(2)}, u32[]{:S(2)}) %collective-permute-start.23) | collective-permute-done | bytes 524320 | tf_op jit(solution)/shard_map/ppermute | solution.py:36
  105.9 2.8 %collective-permute-done.21 = bf16[16,128,128]{2,1,0:T(8,128)(2,1)S(1)} collective-permute-done((bf16[16,128,128]{2,1,0:T(8,128)(2,1)S(1)}, bf16[16,128,128]{2,1,0:T(8,128)(2,1)S(1)}, u32[]{:S(2)}, u32[]{:S(2)}) %collective-permute-start.21) | collective-permute-done | bytes 524320 | tf_op jit(solution)/shard_map/ppermute | solution.py:36
  109.7 2.7 %collective-permute-start.25 = (bf16[16,128,128]{2,1,0:T(8,128)(2,1)}, bf16[16,128,128]{2,1,0:T(8,128)(2,1)}, u32[]{:S(2)}, u32[]{:S(2)}) collective-permute-start(bf16[16,128,128]{2,1,0:T(8,128)(2,1)} %add_convert_fusion.4), channel_id=1, source_target_pairs={{0,196},{1,197},{2,198},{3,199},{8,204},{9,205},{10,206},{11,207},... | collective-permute-start | bytes 1572872 | tf_op jit(solution)/shard_map/ppermute | solution.py:36
  112.5 2.9 %collective-permute-start.19 = (bf16[2,16,8192]{2,1,0:T(8,128)(2,1)S(1)}, bf16[2,16,8192]{2,1,0:T(8,128)(2,1)S(1)}, u32[]{:S(2)}, u32[]{:S(2)}) collective-permute-start(bf16[2,16,8192]{2,1,0:T(8,128)(2,1)S(1)} %get-tuple-element.54), channel_id=1, source_target_pairs={{0,16},{1,17},{2,18},{3,19},{8,24},{9,25},{10,26},{11,27},{16,0},{... | collective-permute-start | bytes 1572872 | tf_op jit(solution)/shard_map/ppermute | solution.py:36
  115.3 7.2 %collective-permute-done.25 = bf16[16,128,128]{2,1,0:T(8,128)(2,1)} collective-permute-done((bf16[16,128,128]{2,1,0:T(8,128)(2,1)}, bf16[16,128,128]{2,1,0:T(8,128)(2,1)}, u32[]{:S(2)}, u32[]{:S(2)}) %collective-permute-start.25) | collective-permute-done | bytes 524320 | tf_op jit(solution)/shard_map/ppermute | solution.py:36
  123.7 2.2 %collective-permute-done.24 = bf16[16,128,128]{2,1,0:T(8,128)(2,1)} collective-permute-done((bf16[16,128,128]{2,1,0:T(8,128)(2,1)}, bf16[16,128,128]{2,1,0:T(8,128)(2,1)}, u32[]{:S(2)}, u32[]{:S(2)}) %collective-permute-start.24) | collective-permute-done | bytes 524320 | tf_op jit(solution)/shard_map/ppermute | solution.py:36
  127.2 3.2 %collective-permute-start.30 = (bf16[16,128,128]{2,1,0:T(8,128)(2,1)S(1)}, bf16[16,128,128]{2,1,0:T(8,128)(2,1)S(1)}, u32[]{:S(2)}, u32[]{:S(2)}) collective-permute-start(bf16[16,128,128]{2,1,0:T(8,128)(2,1)S(1)} %add_convert_fusion.1), channel_id=1, source_target_pairs={{0,196},{1,197},{2,198},{3,199},{8,204},{9,205},{10,206},{11,207},... | collective-permute-start | bytes 1572872 | tf_op jit(solution)/shard_map/ppermute | solution.py:36
  130.9 1.6 %collective-permute-start.26 = (bf16[2,4,8192]{2,1,0:T(4,128)(2,1)S(1)}, bf16[2,4,8192]{2,1,0:T(4,128)(2,1)S(1)}, u32[]{:S(2)}, u32[]{:S(2)}) collective-permute-start(bf16[2,4,8192]{2,1,0:T(4,128)(2,1)S(1)} %get-tuple-element.86), channel_id=1, source_target_pairs={{0,1},{1,2},{2,3},{3,0},{8,9},{9,10},{10,11},{11,8},{16,17},{17,18... | collective-permute-start | bytes 393224 | tf_op jit(solution)/shard_map/ppermute | solution.py:36
  133.8 1.9 %collective-permute-start.28 = (bf16[2,4,8192]{2,1,0:T(4,128)(2,1)S(1)}, bf16[2,4,8192]{2,1,0:T(4,128)(2,1)S(1)}, u32[]{:S(2)}, u32[]{:S(2)}) collective-permute-start(bf16[2,4,8192]{2,1,0:T(4,128)(2,1)S(1)} %get-tuple-element.84), channel_id=1, source_target_pairs={{0,3},{1,0},{2,1},{3,2},{8,11},{9,8},{10,9},{11,10},{16,19},{17,16... | collective-permute-start | bytes 393224 | tf_op jit(solution)/shard_map/ppermute | solution.py:36
  135.7 3.7 %collective-permute-done.29 = bf16[16,128,128]{2,1,0:T(8,128)(2,1)S(1)} collective-permute-done((bf16[16,128,128]{2,1,0:T(8,128)(2,1)S(1)}, bf16[16,128,128]{2,1,0:T(8,128)(2,1)S(1)}, u32[]{:S(2)}, u32[]{:S(2)}) %collective-permute-start.29) | collective-permute-done | bytes 524320 | tf_op jit(solution)/shard_map/ppermute | solution.py:36
  (108 shorter events, 26.4 us)
Async XLA Ops:
  1.9 1.7 %collective-permute-start = (bf16[2,2,2,128,128]{4,3,1,0,2:T(8,128)(2,1)S(1)}, bf16[2,2,2,128,128]{4,3,1,0,2:T(8,128)(2,1)S(1)}, u32[]{:S(2)}, u32[]{:S(2)}) collective-permute-start(bf16[2,2,2,128,128]{4,3,1,0,2:T(8,128)(2,1)S(1)} %get-tuple-element.89), channel_id=1, source_target_pairs={{0,32},{1,33},{2,34},{3,35},{8,40},{9,41},{10,42},{11,43},{16,48},... | collective-permute-start | bytes 786440 | tf_op jit(solution)/shard_map/ppermute | solution.py:36
  3.7 18.6 %collective-permute-start.1 = (bf16[2064,128]{1,0:T(8,128)(2,1)S(1)}, bf16[2064,128]{1,0:T(8,128)(2,1)S(1)}, u32[]{:S(2)}, u32[]{:S(2)}) collective-permute-start(bf16[2064,128]{1,0:T(8,128)(2,1)S(1)} %fusion.1.refs_5_), channel_id=1, source_target_pairs={{0,64},{1,65},{2,66},{3,67},{8,72},{9,73},{10,74},{11,75},{16,80},... | collective-permute-start | bytes 1585160 | tf_op jit(solution)/shard_map/ppermute | solution.py:36
  5.7 16.6 %collective-permute-start.2 = (bf16[2064,128]{1,0:T(8,128)(2,1)S(1)}, bf16[2064,128]{1,0:T(8,128)(2,1)S(1)}, u32[]{:S(2)}, u32[]{:S(2)}) collective-permute-start(bf16[2064,128]{1,0:T(8,128)(2,1)S(1)} %fusion.1.refs_5_), channel_id=1, source_target_pairs={{0,196},{1,197},{2,198},{3,199},{8,204},{9,205},{10,206},{11,207},... | collective-permute-start | bytes 1585160 | tf_op jit(solution)/shard_map/ppermute | solution.py:36
  9.9 5.7 %collective-permute-start.3 = (bf16[2,4,8192]{2,1,0:T(4,128)(2,1)S(1)}, bf16[2,4,8192]{2,1,0:T(4,128)(2,1)S(1)}, u32[]{:S(2)}, u32[]{:S(2)}) collective-permute-start(bf16[2,4,8192]{2,1,0:T(4,128)(2,1)S(1)} %pad_maximum_fusion.1), channel_id=1, source_target_pairs={{0,3},{1,0},{2,1},{3,2},{8,11},{9,8},{10,9},{11,10},{16,19},{17,16... | collective-permute-start | bytes 393224 | tf_op jit(solution)/shard_map/ppermute | solution.py:36
  10.5 8.8 %collective-permute-start.4 = (bf16[2,4,8192]{2,1,0:T(4,128)(2,1)S(1)}, bf16[2,4,8192]{2,1,0:T(4,128)(2,1)S(1)}, u32[]{:S(2)}, u32[]{:S(2)}) collective-permute-start(bf16[2,4,8192]{2,1,0:T(4,128)(2,1)S(1)} %pad_maximum_fusion.1), channel_id=1, source_target_pairs={{0,2},{1,3},{2,0},{3,1},{8,10},{9,11},{10,8},{11,9},{16,18},{17,19... | collective-permute-start | bytes 393224 | tf_op jit(solution)/shard_map/ppermute | solution.py:36
  12.9 7.3 %collective-permute-start.5 = (bf16[2,4,8192]{2,1,0:T(4,128)(2,1)S(1)}, bf16[2,4,8192]{2,1,0:T(4,128)(2,1)S(1)}, u32[]{:S(2)}, u32[]{:S(2)}) collective-permute-start(bf16[2,4,8192]{2,1,0:T(4,128)(2,1)S(1)} %pad_maximum_fusion.1), channel_id=1, source_target_pairs={{0,1},{1,2},{2,3},{3,0},{8,9},{9,10},{10,11},{11,8},{16,17},{17,18... | collective-permute-start | bytes 393224 | tf_op jit(solution)/shard_map/ppermute | solution.py:36
  22.7 15.1 %collective-permute-start.6 = (bf16[2064,128]{1,0:T(8,128)(2,1)S(1)}, bf16[2064,128]{1,0:T(8,128)(2,1)S(1)}, u32[]{:S(2)}, u32[]{:S(2)}) collective-permute-start(bf16[2064,128]{1,0:T(8,128)(2,1)S(1)} %collective-permute-done.1.refs_9_), channel_id=1, source_target_pairs={{0,64},{1,65},{2,66},{3,67},{8,72},{9,73},{10,74},{11,75},{16,80},... | collective-permute-start | bytes 1585160 | tf_op jit(solution)/shard_map/ppermute | solution.py:36
  22.8 15.0 %collective-permute-start.7 = (bf16[2064,128]{1,0:T(8,128)(2,1)S(1)}, bf16[2064,128]{1,0:T(8,128)(2,1)S(1)}, u32[]{:S(2)}, u32[]{:S(2)}) collective-permute-start(bf16[2064,128]{1,0:T(8,128)(2,1)S(1)} %collective-permute-done.2.refs_6_), channel_id=1, source_target_pairs={{0,196},{1,197},{2,198},{3,199},{8,204},{9,205},{10,206},{11,207},... | collective-permute-start | bytes 1585160 | tf_op jit(solution)/shard_map/ppermute | solution.py:36
  26.0 15.0 %collective-permute-start.10 = (bf16[2,16,8192]{2,1,0:T(8,128)(2,1)S(1)}, bf16[2,16,8192]{2,1,0:T(8,128)(2,1)S(1)}, u32[]{:S(2)}, u32[]{:S(2)}) collective-permute-start(bf16[2,16,8192]{2,1,0:T(8,128)(2,1)S(1)} %pad_maximum_fusion), channel_id=1, source_target_pairs={{0,8},{1,9},{2,10},{3,11},{8,16},{9,17},{10,18},{11,19},{16,24},{1... | collective-permute-start | bytes 1572872 | tf_op jit(solution)/shard_map/ppermute | solution.py:36
  27.6 14.9 %collective-permute-start.8 = (bf16[2,16,8192]{2,1,0:T(8,128)(2,1)S(1)}, bf16[2,16,8192]{2,1,0:T(8,128)(2,1)S(1)}, u32[]{:S(2)}, u32[]{:S(2)}) collective-permute-start(bf16[2,16,8192]{2,1,0:T(8,128)(2,1)S(1)} %pad_maximum_fusion), channel_id=1, source_target_pairs={{0,24},{1,25},{2,26},{3,27},{8,0},{9,1},{10,2},{11,3},{16,8},{17,9... | collective-permute-start | bytes 1572872 | tf_op jit(solution)/shard_map/ppermute | solution.py:36
  29.2 23.6 %collective-permute-start.9 = (bf16[2,16,8192]{2,1,0:T(8,128)(2,1)S(1)}, bf16[2,16,8192]{2,1,0:T(8,128)(2,1)S(1)}, u32[]{:S(2)}, u32[]{:S(2)}) collective-permute-start(bf16[2,16,8192]{2,1,0:T(8,128)(2,1)S(1)} %pad_maximum_fusion), channel_id=1, source_target_pairs={{0,16},{1,17},{2,18},{3,19},{8,24},{9,25},{10,26},{11,27},{16,0},{... | collective-permute-start | bytes 1572872 | tf_op jit(solution)/shard_map/ppermute | solution.py:36
  37.8 15.0 %collective-permute-start.11 = (bf16[2048,128]{1,0:T(8,128)(2,1)S(1)}, bf16[2048,128]{1,0:T(8,128)(2,1)S(1)}, u32[]{:S(2)}, u32[]{:S(2)}) collective-permute-start(bf16[2048,128]{1,0:T(8,128)(2,1)S(1)} %slice.89), channel_id=1, source_target_pairs={{0,196},{1,197},{2,198},{3,199},{8,204},{9,205},{10,206},{11,207},... | collective-permute-start | bytes 1572872 | tf_op jit(solution)/shard_map/ppermute | solution.py:36
  40.9 13.7 %collective-permute-start.12 = (bf16[2048,128]{1,0:T(8,128)(2,1)S(1)}, bf16[2048,128]{1,0:T(8,128)(2,1)}, u32[]{:S(2)}, u32[]{:S(2)}) collective-permute-start(bf16[2048,128]{1,0:T(8,128)(2,1)S(1)} %slice.90), channel_id=1, source_target_pairs={{0,64},{1,65},{2,66},{3,67},{8,72},{9,73},{10,74},{11,75},{16,80},... | collective-permute-start | bytes 1572872 | tf_op jit(solution)/shard_map/ppermute | solution.py:36
  54.8 13.3 %collective-permute-start.13 = (bf16[2,64,8192]{2,1,0:T(8,128)(2,1)S(1)}, bf16[2,64,8192]{2,1,0:T(8,128)(2,1)}, u32[]{:S(2)}, u32[]{:S(2)}) collective-permute-start(bf16[2,64,8192]{2,1,0:T(8,128)(2,1)S(1)} %constant_dynamic-update-slice_fusion.refs_3_), channel_id=1, source_target_pairs={{0,32},{1,33},{2,34},{3,35},{8,40},{9,41},{10,42},{11,43},{16,48},... | collective-permute-start | bytes 6291464 | tf_op jit(solution)/shard_map/ppermute | solution.py:36
  56.6 8.7 %collective-permute-start.14 = (bf16[1024,128]{1,0:T(8,128)(2,1)S(1)}, bf16[1024,128]{1,0:T(8,128)(2,1)S(1)}, u32[]{:S(2)}, u32[]{:S(2)}) collective-permute-start(bf16[1024,128]{1,0:T(8,128)(2,1)S(1)} %slice.113), channel_id=1, source_target_pairs={{0,196},{1,197},{2,198},{3,199},{8,204},{9,205},{10,206},{11,207},... | collective-permute-start | bytes 786440 | tf_op jit(solution)/shard_map/ppermute | solution.py:36
  58.2 9.9 %collective-permute-start.15 = (bf16[1024,128]{1,0:T(8,128)(2,1)S(1)}, bf16[1024,128]{1,0:T(8,128)(2,1)S(1)}, u32[]{:S(2)}, u32[]{:S(2)}) collective-permute-start(bf16[1024,128]{1,0:T(8,128)(2,1)S(1)} %slice.114), channel_id=1, source_target_pairs={{0,64},{1,65},{2,66},{3,67},{8,72},{9,73},{10,74},{11,75},{16,80},... | collective-permute-start | bytes 786440 | tf_op jit(solution)/shard_map/ppermute | solution.py:36
  81.3 13.5 %collective-permute-start.16 = (bf16[2,64,8192]{2,1,0:T(8,128)(2,1)}, bf16[2,64,8192]{2,1,0:T(8,128)(2,1)S(1)}, u32[]{:S(2)}, u32[]{:S(2)}) collective-permute-start(bf16[2,64,8192]{2,1,0:T(8,128)(2,1)} %get-tuple-element.53), channel_id=1, source_target_pairs={{0,32},{1,33},{2,34},{3,35},{8,40},{9,41},{10,42},{11,43},{16,48},... | collective-permute-start | bytes 6291464 | tf_op jit(solution)/shard_map/ppermute | solution.py:36
  81.4 8.9 %collective-permute-start.22 = (bf16[8,128,128]{2,1,0:T(8,128)(2,1)}, bf16[8,128,128]{2,1,0:T(8,128)(2,1)S(1)}, u32[]{:S(2)}, u32[]{:S(2)}) collective-permute-start(bf16[8,128,128]{2,1,0:T(8,128)(2,1)} %get-tuple-element.60), channel_id=1, source_target_pairs={{0,196},{1,197},{2,198},{3,199},{8,204},{9,205},{10,206},{11,207},... | collective-permute-start | bytes 786440 | tf_op jit(solution)/shard_map/ppermute | solution.py:36
  81.5 11.5 %collective-permute-start.20 = (bf16[8,128,128]{2,1,0:T(8,128)(2,1)}, bf16[8,128,128]{2,1,0:T(8,128)(2,1)S(1)}, u32[]{:S(2)}, u32[]{:S(2)}) collective-permute-start(bf16[8,128,128]{2,1,0:T(8,128)(2,1)} %get-tuple-element.57), channel_id=1, source_target_pairs={{0,64},{1,65},{2,66},{3,67},{8,72},{9,73},{10,74},{11,75},{16,80},... | collective-permute-start | bytes 786440 | tf_op jit(solution)/shard_map/ppermute | solution.py:36
  91.4 13.6 %collective-permute-start.23 = (bf16[16,128,128]{2,1,0:T(8,128)(2,1)S(1)}, bf16[16,128,128]{2,1,0:T(8,128)(2,1)S(1)}, u32[]{:S(2)}, u32[]{:S(2)}) collective-permute-start(bf16[16,128,128]{2,1,0:T(8,128)(2,1)S(1)} %add_convert_fusion.5), channel_id=1, source_target_pairs={{0,196},{1,197},{2,198},{3,199},{8,204},{9,205},{10,206},{11,207},... | collective-permute-start | bytes 1572872 | tf_op jit(solution)/shard_map/ppermute | solution.py:36
  94.1 14.7 %collective-permute-start.21 = (bf16[16,128,128]{2,1,0:T(8,128)(2,1)S(1)}, bf16[16,128,128]{2,1,0:T(8,128)(2,1)S(1)}, u32[]{:S(2)}, u32[]{:S(2)}) collective-permute-start(bf16[16,128,128]{2,1,0:T(8,128)(2,1)S(1)} %add_convert_fusion.7), channel_id=1, source_target_pairs={{0,64},{1,65},{2,66},{3,67},{8,72},{9,73},{10,74},{11,75},{16,80},... | collective-permute-start | bytes 1572872 | tf_op jit(solution)/shard_map/ppermute | solution.py:36
  95.3 14.5 %collective-permute-start.17 = (bf16[2,16,8192]{2,1,0:T(8,128)(2,1)S(1)}, bf16[2,16,8192]{2,1,0:T(8,128)(2,1)S(1)}, u32[]{:S(2)}, u32[]{:S(2)}) collective-permute-start(bf16[2,16,8192]{2,1,0:T(8,128)(2,1)S(1)} %get-tuple-element.78), channel_id=1, source_target_pairs={{0,8},{1,9},{2,10},{3,11},{8,16},{9,17},{10,18},{11,19},{16,24},{1... | collective-permute-start | bytes 1572872 | tf_op jit(solution)/shard_map/ppermute | solution.py:36
  96.9 12.8 %collective-permute-start.18 = (bf16[2,16,8192]{2,1,0:T(8,128)(2,1)S(1)}, bf16[2,16,8192]{2,1,0:T(8,128)(2,1)S(1)}, u32[]{:S(2)}, u32[]{:S(2)}) collective-permute-start(bf16[2,16,8192]{2,1,0:T(8,128)(2,1)S(1)} %get-tuple-element.77), channel_id=1, source_target_pairs={{0,24},{1,25},{2,26},{3,27},{8,0},{9,1},{10,2},{11,3},{16,8},{17,9... | collective-permute-start | bytes 1572872 | tf_op jit(solution)/shard_map/ppermute | solution.py:36
  109.7 12.8 %collective-permute-start.25 = (bf16[16,128,128]{2,1,0:T(8,128)(2,1)}, bf16[16,128,128]{2,1,0:T(8,128)(2,1)}, u32[]{:S(2)}, u32[]{:S(2)}) collective-permute-start(bf16[16,128,128]{2,1,0:T(8,128)(2,1)} %add_convert_fusion.4), channel_id=1, source_target_pairs={{0,196},{1,197},{2,198},{3,199},{8,204},{9,205},{10,206},{11,207},... | collective-permute-start | bytes 1572872 | tf_op jit(solution)/shard_map/ppermute | solution.py:36
  112.4 13.4 %collective-permute-start.24 = (bf16[16,128,128]{2,1,0:T(8,128)(2,1)}, bf16[16,128,128]{2,1,0:T(8,128)(2,1)}, u32[]{:S(2)}, u32[]{:S(2)}) collective-permute-start(bf16[16,128,128]{2,1,0:T(8,128)(2,1)} %add_convert_fusion.6), channel_id=1, source_target_pairs={{0,64},{1,65},{2,66},{3,67},{8,72},{9,73},{10,74},{11,75},{16,80},... | collective-permute-start | bytes 1572872 | tf_op jit(solution)/shard_map/ppermute | solution.py:36
  112.5 14.6 %collective-permute-start.19 = (bf16[2,16,8192]{2,1,0:T(8,128)(2,1)S(1)}, bf16[2,16,8192]{2,1,0:T(8,128)(2,1)S(1)}, u32[]{:S(2)}, u32[]{:S(2)}) collective-permute-start(bf16[2,16,8192]{2,1,0:T(8,128)(2,1)S(1)} %get-tuple-element.54), channel_id=1, source_target_pairs={{0,16},{1,17},{2,18},{3,19},{8,24},{9,25},{10,26},{11,27},{16,0},{... | collective-permute-start | bytes 1572872 | tf_op jit(solution)/shard_map/ppermute | solution.py:36
  127.1 12.3 %collective-permute-start.29 = (bf16[16,128,128]{2,1,0:T(8,128)(2,1)S(1)}, bf16[16,128,128]{2,1,0:T(8,128)(2,1)S(1)}, u32[]{:S(2)}, u32[]{:S(2)}) collective-permute-start(bf16[16,128,128]{2,1,0:T(8,128)(2,1)S(1)} %add_convert_fusion.2), channel_id=1, source_target_pairs={{0,64},{1,65},{2,66},{3,67},{8,72},{9,73},{10,74},{11,75},{16,80},... | collective-permute-start | bytes 1572872 | tf_op jit(solution)/shard_map/ppermute | solution.py:36
  127.2 12.2 %collective-permute-start.30 = (bf16[16,128,128]{2,1,0:T(8,128)(2,1)S(1)}, bf16[16,128,128]{2,1,0:T(8,128)(2,1)S(1)}, u32[]{:S(2)}, u32[]{:S(2)}) collective-permute-start(bf16[16,128,128]{2,1,0:T(8,128)(2,1)S(1)} %add_convert_fusion.1), channel_id=1, source_target_pairs={{0,196},{1,197},{2,198},{3,199},{8,204},{9,205},{10,206},{11,207},... | collective-permute-start | bytes 1572872 | tf_op jit(solution)/shard_map/ppermute | solution.py:36
  130.9 9.0 %collective-permute-start.26 = (bf16[2,4,8192]{2,1,0:T(4,128)(2,1)S(1)}, bf16[2,4,8192]{2,1,0:T(4,128)(2,1)S(1)}, u32[]{:S(2)}, u32[]{:S(2)}) collective-permute-start(bf16[2,4,8192]{2,1,0:T(4,128)(2,1)S(1)} %get-tuple-element.86), channel_id=1, source_target_pairs={{0,1},{1,2},{2,3},{3,0},{8,9},{9,10},{10,11},{11,8},{16,17},{17,18... | collective-permute-start | bytes 393224 | tf_op jit(solution)/shard_map/ppermute | solution.py:36
  132.4 7.4 %collective-permute-start.27 = (bf16[2,4,8192]{2,1,0:T(4,128)(2,1)S(1)}, bf16[2,4,8192]{2,1,0:T(4,128)(2,1)S(1)}, u32[]{:S(2)}, u32[]{:S(2)}) collective-permute-start(bf16[2,4,8192]{2,1,0:T(4,128)(2,1)S(1)} %get-tuple-element.85), channel_id=1, source_target_pairs={{0,2},{1,3},{2,0},{3,1},{8,10},{9,11},{10,8},{11,9},{16,18},{17,19... | collective-permute-start | bytes 393224 | tf_op jit(solution)/shard_map/ppermute | solution.py:36
  133.8 6.4 %collective-permute-start.28 = (bf16[2,4,8192]{2,1,0:T(4,128)(2,1)S(1)}, bf16[2,4,8192]{2,1,0:T(4,128)(2,1)S(1)}, u32[]{:S(2)}, u32[]{:S(2)}) collective-permute-start(bf16[2,4,8192]{2,1,0:T(4,128)(2,1)S(1)} %get-tuple-element.84), channel_id=1, source_target_pairs={{0,3},{1,0},{2,1},{3,2},{8,11},{9,8},{10,9},{11,10},{16,19},{17,16... | collective-permute-start | bytes 393224 | tf_op jit(solution)/shard_map/ppermute | solution.py:36
  139.7 1.6 %collective-permute-start.31 = (bf16[2,2,2,128,128]{4,3,1,0,2:T(8,128)(2,1)S(1)}, bf16[2,2,2,128,128]{4,3,1,0,2:T(8,128)(2,1)S(1)}, u32[]{:S(2)}, u32[]{:S(2)}) collective-permute-start(bf16[2,2,2,128,128]{4,3,1,0,2:T(8,128)(2,1)S(1)} %bitcast.34), channel_id=1, source_target_pairs={{0,32},{1,33},{2,34},{3,35},{8,40},{9,41},{10,42},{11,43},{16,48},... | collective-permute-start | bytes 786440 | tf_op jit(solution)/shard_map/ppermute | solution.py:36
  (18 other events, 276.0 us)
